TPU v7x, 32 devices: a whole 2x2x4 slice. The times are simulated.
32 devices in a mesh: grp: 2 (over x), lon: 16 (over z, y, core), lat: 1.
Axes of the slice: x: 2, y: 2, z: 4, core: 2. Of those that a mesh axis runs over, the one named last changes fastest.
Arguments:
- tokens: bfloat16 [4, 8, 128, 1536], P('grp', 'lat', 'lon'), parts along dimension 0, may hold values from -6 to 6
- land: int32 [16, 128], P(('grp', 'lat'), 'lon'), parts along dimension 0, may hold values 0 or 1
- surface: float32 [2, 1536], replicated, may hold values from -4 to 4
- gain: float32 [1536], replicated, may hold values from 0.25 to 1.75
- weights: bfloat16 [1536, 3072], P('lon'), may hold values from -0.15625 to 0.15625
- shifts: int32 [2, 2], replicated, may hold values from 1 to 7, as said below
- index_table: int32 [64, 64], replicated, may hold values from 0 to 224
- bias_table: float32 [2, 225, 12], P('lat'), as said below
- cotangent: bfloat16 [4, 8, 128, 1536], P('grp', 'lat', 'lon'), parts along dimension 0, may hold values from -6 to 6
Outputs:
- output: bfloat16 [4, 8, 128, 1536], P('grp', 'lat', 'lon'), parts along dimension 0
- grad_tokens: bfloat16 [4, 8, 128, 1536], P('grp', 'lat', 'lon'), parts along dimension 0
- grad_weights: float32 [3072, 3072], P(('grp', 'lon')), parts along dimension 0
There are 2 independent parts, one for each index of `grp`. A program takes and returns all parts, laid end to end along the dimension named above; an argument that names none is the same for every part. Nothing has to cross between parts.
Inputs may be any that keep to these rules, and one draw needn't show every extreme that they name: `shifts`: row l holds level l's offsets along latitude and longitude; taken together the entries include 1 and 7. `bias_table`: every entry is finite.
All inputs are finite; a program needn't handle non-finite values. No bound on the sum of `land` on one device may be relied on, other than what follows from the above.
Results may differ from a plain program's by a relative error of at most 0.023.
Values may be sent and summed in bfloat16 or wider, within the bound.
No kernel may reach another device: no remote copies, remote signals or barrier semaphores. Data moves between devices by JAX's collectives and lax.ppermute only.
A program may use at most 128 MiB of HBM per device.

v0:
```python
import math

import jax
import jax.numpy as jnp
from jax import lax
from jax.sharding import PartitionSpec as P

epsilon = 1e-05


def passed_along(shard, axis, by):
    count = lax.axis_size(axis)
    return lax.ppermute(shard, axis, [(i, (i + by) % count) for i in range(count)])


def normalize(stream, gain):
    values = stream.astype(jnp.float32)
    center = values - jnp.mean(values, axis=-1, keepdims=True)
    spread = lax.rsqrt(jnp.mean(center * center, axis=-1, keepdims=True) + epsilon)
    return (center * spread * gain).astype(jnp.bfloat16)


def normalize_back(stream, gain, grad_normed):
    values = stream.astype(jnp.float32)
    center = values - jnp.mean(values, axis=-1, keepdims=True)
    spread = lax.rsqrt(jnp.mean(center * center, axis=-1, keepdims=True) + epsilon)
    scaled = center * spread
    upstream = grad_normed.astype(jnp.float32) * gain
    return spread * (
        upstream
        - jnp.mean(upstream, axis=-1, keepdims=True)
        - scaled * jnp.mean(upstream * scaled, axis=-1, keepdims=True)
    )


def take_levels(field, starts, axis, length):

    def one_level(plane, start):
        return lax.dynamic_slice_in_dim(plane, start, length, axis - 1)

    return jax.vmap(one_level, in_axes=(1, 0), out_axes=1)(field, starts)


def roll_forward(field, shifts):
    tile_rows = field.shape[2]
    tile_cols = field.shape[3]
    below = passed_along(field, "lat", -1)
    rows_done = take_levels(jnp.concatenate([field, below], axis=2), shifts[:, 0], 2, tile_rows)
    beside = passed_along(rows_done, "lon", -1)
    return take_levels(jnp.concatenate([rows_done, beside], axis=3), shifts[:, 1], 3, tile_cols)


def roll_back(field, shifts):
    tile_rows = field.shape[2]
    tile_cols = field.shape[3]
    before = passed_along(field, "lon", 1)
    cols_done = take_levels(
        jnp.concatenate([before, field], axis=3), tile_rows - shifts[:, 1], 3, tile_cols
    )
    above = passed_along(cols_done, "lat", 1)
    return take_levels(
        jnp.concatenate([above, cols_done], axis=2), tile_rows - shifts[:, 0], 2, tile_rows
    )


def attend_forward(normed, w_qkv, w_out, bias_tile, allowed, heads):
    levels, tile_rows, tile_cols, model_width = normed.shape
    windows = tile_cols // tile_rows
    area = tile_rows * tile_rows
    qkv = jnp.dot(
        normed.reshape(-1, model_width), w_qkv, preferred_element_type=jnp.float32
    ).astype(jnp.bfloat16)
    view = qkv.reshape(levels, tile_rows, windows, tile_rows, 3, heads, -1)
    query = view[:, :, :, :, 0]
    keys = view[:, :, :, :, 1]
    values = view[:, :, :, :, 2]
    head_size = query.shape[-1]
    scale = 1.0 / math.sqrt(head_size)
    scores = jnp.einsum("lawbhd,lcwehd->lwhabce", query, keys, preferred_element_type=jnp.float32)
    scores = scores.reshape(levels, windows, heads, area, area) * scale + bias_tile[:, None]
    scores = jnp.where(allowed[:, None, None], scores, -1e30)
    top = jnp.max(scores, axis=-1, keepdims=True)
    expo = jnp.exp(scores - top)
    probs = expo / jnp.sum(expo, axis=-1, keepdims=True)
    probs_b = probs.astype(jnp.bfloat16).reshape(
        levels, windows, heads, tile_rows, tile_rows, tile_rows, tile_rows
    )
    mixed = jnp.einsum(
        "lwhabce,lcwehd->lawbhd", probs_b, values, preferred_element_type=jnp.float32
    )
    mixed_flat = mixed.astype(jnp.bfloat16).reshape(-1, heads * head_size)
    attended = lax.dot_general(
        mixed_flat, w_out, (((1,), (1,)), ((), ())), preferred_element_type=jnp.float32
    )
    attended = attended.astype(jnp.bfloat16).reshape(levels, tile_rows, tile_cols, model_width)
    return ((query, keys, values, probs, probs_b, mixed_flat), attended)


def attend_backward(rolled_cot, saved, w_qkv, w_out):
    query, keys, values, probs, probs_b, mixed_flat = saved
    levels, tile_rows, tile_cols, model_width = rolled_cot.shape
    heads = query.shape[4]
    head_size = query.shape[5]
    scale = 1.0 / math.sqrt(head_size)
    grad_mixed = jnp.dot(
        rolled_cot.reshape(-1, model_width), w_out, preferred_element_type=jnp.float32
    )
    grad_mixed = grad_mixed.astype(jnp.bfloat16).reshape(query.shape)
    grad_probs = jnp.einsum(
        "lawbhd,lcwehd->lwhabce", grad_mixed, values, preferred_element_type=jnp.float32
    )
    grad_probs = grad_probs.reshape(probs.shape)
    grad_values = jnp.einsum(
        "lwhabce,lawbhd->lcwehd", probs_b, grad_mixed, preferred_element_type=jnp.float32
    )
    grad_values = grad_values.astype(jnp.bfloat16)
    grad_scores = probs * (grad_probs - jnp.sum(probs * grad_probs, axis=-1, keepdims=True))
    grad_scores = (grad_scores * scale).astype(jnp.bfloat16).reshape(probs_b.shape)
    grad_query = jnp.einsum(
        "lwhabce,lcwehd->lawbhd", grad_scores, keys, preferred_element_type=jnp.float32
    )
    grad_keys = jnp.einsum(
        "lwhabce,lawbhd->lcwehd", grad_scores, query, preferred_element_type=jnp.float32
    )
    grad_qkv = jnp.stack(
        [grad_query.astype(jnp.bfloat16), grad_keys.astype(jnp.bfloat16), grad_values], axis=4
    )
    grad_qkv = grad_qkv.reshape(-1, 3 * heads * head_size)
    grad_normed = lax.dot_general(
        grad_qkv, w_qkv, (((1,), (1,)), ((), ())), preferred_element_type=jnp.float32
    )
    grad_normed = grad_normed.astype(jnp.bfloat16).reshape(
        levels, tile_rows, tile_cols, model_width
    )
    return (grad_normed, grad_qkv)


def on_device(tokens, land, surface, gain, weights, shifts, index_table, bias_table, cotangent):
    levels, tile_rows, tile_cols, model_width = tokens.shape
    heads = bias_table.shape[2]
    entries = bias_table.shape[1]
    proj_width = weights.shape[1] // 4
    full_weights = lax.all_gather(weights, "lon", axis=0, tiled=True)
    w_qkv = full_weights[:, : 3 * proj_width]
    w_out = full_weights[:, 3 * proj_width :]
    surface_term = jnp.where(land[None, :, :, None] == 1, surface[1], surface[0])
    stream = (tokens.astype(jnp.float32) + surface_term).astype(jnp.bfloat16)
    onehot = (index_table[:, :, None] == jnp.arange(entries, dtype=jnp.int32)).astype(jnp.float32)
    bias_tile = jnp.einsum("qkr,lrh->lhqk", onehot, bias_table, precision=lax.Precision.HIGHEST)
    total_rows = tile_rows * lax.axis_size("lat")
    row_number = lax.axis_index("lat") * tile_rows + jnp.arange(tile_rows, dtype=jnp.int32)
    group = row_number[None, :] >= (total_rows - shifts[:, 0])[:, None]
    group = jnp.repeat(group, tile_rows, axis=1)
    allowed = group[:, :, None] == group[:, None, :]
    normed = roll_forward(normalize(stream, gain)[None], shifts)[0]
    saved, attended = attend_forward(normed, w_qkv, w_out, bias_tile, allowed, heads)
    attended = roll_back(attended[None], shifts)[0]
    output = (stream.astype(jnp.float32) + attended.astype(jnp.float32)).astype(jnp.bfloat16)
    rolled_cot = roll_forward(cotangent[None], shifts)[0]
    grad_normed, grad_qkv = attend_backward(rolled_cot, saved, w_qkv, w_out)
    grad_normed = roll_back(grad_normed[None], shifts)[0]
    grad_stream = normalize_back(stream, gain, grad_normed)
    grad_tokens = (cotangent.astype(jnp.float32) + grad_stream).astype(jnp.bfloat16)
    flat_normed = normed.reshape(-1, model_width)
    flat_cot = rolled_cot.reshape(-1, model_width)
    mixed_flat = saved[5]
    first = lax.dot_general(
        flat_normed, grad_qkv, (((0,), (0,)), ((), ())), preferred_element_type=jnp.float32
    )
    second = lax.dot_general(
        flat_cot, mixed_flat, (((0,), (0,)), ((), ())), preferred_element_type=jnp.float32
    )
    grad_rows = lax.psum_scatter(
        jnp.concatenate([first, second], axis=1).astype(jnp.bfloat16),
        "lon",
        scatter_dimension=0,
        tiled=True,
    )
    summed = lax.psum(grad_rows, "lat").astype(jnp.float32)
    token_count = levels * tile_rows * lax.axis_size("lat") * tile_cols * lax.axis_size("lon")
    grad_weights = summed * (1.0 / math.sqrt(token_count))
    return (output, grad_tokens, grad_weights)


def solution(mesh):
    return jax.shard_map(
        on_device,
        mesh=mesh,
        in_specs=(
            P("grp", "lat", "lon", None),
            P(("grp", "lat"), "lon"),
            P(),
            P(),
            P("lon", None),
            P(),
            P(),
            P("lat", None, None),
            P("grp", "lat", "lon", None),
        ),
        out_specs=(
            P("grp", "lat", "lon", None),
            P("grp", "lat", "lon", None),
            P(("grp", "lon"), None),
        ),
        check_vma=False,
    )
```

profile of v0, /device:TPU:6, one launch (start us, length us, event | category | flops | bytes accessed | tf_op | source)
XLA Modules:
  0.0 314.9 jit_solution(16213481077203317431)
XLA Ops:
  10.6 1.2 convert_reduce_fusion
  16.4 3.2 %collective-permute-done.5 = bf16[1,2,8,8,1536]{4,3,2,1,0:T(8,128)(2,1)S(1)} collective-permute-done((bf16[1,2,8,8,1536]{4,3,2,1,0:T(8,128)(2,1)S(1)}, bf16[1,2,8,8,1536]{4,3,2,1,0:T(8,128)(2,1)S(1)}, u32[]{:S(2)}, u32[]{:S(2)}) %collective-permute-start.5) | collective-permute-done | bytes 393248 | tf_op jit(solution)/shard_map/ppermute | solution.py:13
  20.9 9.3 %collective-permute-done.1 = bf16[1,2,8,8,1536]{4,3,2,1,0:T(8,128)(2,1)S(1)} collective-permute-done((bf16[1,2,8,8,1536]{4,3,2,1,0:T(8,128)(2,1)S(1)}, bf16[1,2,8,8,1536]{4,3,2,1,0:T(8,128)(2,1)S(1)}, u32[]{:S(2)}, u32[]{:S(2)}) %collective-permute-start.1) | collective-permute-done | bytes 393248 | tf_op jit(solution)/shard_map/ppermute | solution.py:13
  31.4 66.7 %all-gather.2.cloned.1.call-done = bf16[1536,3072]{1,0:T(8,128)(2,1)} async-done(((bf16[96,3072]{1,0:T(8,128)(2,1)}), bf16[1536,3072]{1,0:T(8,128)(2,1)}) %all-gather.2.cloned.1.call-update) | async-done | bytes 9437200 | tf_op jit(solution)/shard_map/all_gather | solution.py:143
  98.1 2.1 fusion.78
  100.6 4.3 %fusion.9 = bf16[128,2304]{1,0:T(8,128)(2,1)S(1)} fusion(bf16[128,1536]{1,0:T(8,128)(2,1)S(1)} %bitcast.157, bf16[1536,3072]{1,0:T(8,128)(2,1)} %all-gather.2.cloned.1.call-done), kind=kOutput, calls=%fused_computation.19 | convolution fusion | flops 906264576 | bytes 8060928 | tf_op jit(solution)/shard_map/dot_general | solution.py:70
  104.9 1.2 reshape.142
  107.2 2.4 fusion.101
  109.6 3.8 %copy.96 = f32[2,12,8,8,8,8]{5,4,1,0,3,2:T(8,128)} copy(f32[2,12,8,8,8,8]{5,3,4,2,1,0:T(8,128)S(1)} %fusion.101) | data formatting | bytes 786432 | tf_op jit(solution)/shard_map/reshape | solution.py:112
  113.4 4.3 %reshape.232 = f32[2,12,64,64]{3,1,0,2:T(8,128)S(1)} reshape(f32[2,12,8,8,8,8]{5,4,1,0,3,2:T(8,128)} %copy.96) | data formatting | bytes 786432 | tf_op jit(solution)/shard_map/reshape | solution.py:112
  117.8 2.4 broadcast_multiply_fusion
  120.1 3.8 %copy.90 = f32[2,12,8,8,8,8]{5,4,1,0,3,2:T(8,128)} copy(f32[2,12,8,8,8,8]{5,3,4,2,1,0:T(8,128)S(1)} %broadcast_multiply_fusion) | data formatting | bytes 786432 | tf_op jit(solution)/shard_map/mul | solution.py:80
  124.0 4.3 %reshape.231 = f32[2,12,64,64]{3,1,0,2:T(8,128)S(1)} reshape(f32[2,12,8,8,8,8]{5,4,1,0,3,2:T(8,128)} %copy.90) | data formatting | bytes 786432 | tf_op jit(solution)/shard_map/mul | solution.py:80
  128.3 3.0 fusion.35
  131.3 21.7 %fusion.125 = (f32[2,12,64]{1,0,2:T(2,128)S(1)}, f32[2,12,64,64]{3,1,0,2:T(8,128)S(1)}) fusion(f32[2,12,64,64]{3,1,0,2:T(8,128)S(1)} %fusion.35), kind=kOutput, calls=%fused_computation.138 | output fusion | flops 196671 | bytes 792576 | tf_op jit(solution)/shard_map/sub | solution.py:83
  154.1 11.2 %fusion.53 = bf16[2,12,64,64]{3,1,0,2:T(8,128)(2,1)S(1)} fusion(f32[2,12,64,64]{3,1,0,2:T(8,128)S(1)} %reshape.232, f32[2,12,64,64]{3,1,0,2:T(8,128)S(1)} %get-tuple-element.26, f32[2,12,64]{1,0,2:T(2,128)S(1)} %get-tuple-element.25), kind=kOutput, calls=%fused_computation.48 | output fusion | flops 689727 | bytes 989184 | tf_op jit(solution)/shard_map/sub | solution.py:117
  166.2 3.5 %reshape.150 = bf16[2,12,8,8,8,8]{5,4,3,2,1,0:T(8,128)(2,1)S(1)} reshape(bf16[2,12,64,64]{3,2,1,0:T(8,128)(2,1)} %copy.65) | data formatting | bytes 393216 | tf_op jit(solution)/shard_map/reshape.30
  169.7 2.8 fusion.72
  172.5 2.3 fusion.69
  175.8 3.5 %reshape.146 = bf16[2,12,8,8,8,8]{5,4,3,2,1,0:T(8,128)(2,1)S(1)} reshape(bf16[2,12,64,64]{3,2,1,0:T(8,128)(2,1)} %copy.50) | data formatting | bytes 393216 | tf_op jit(solution)/shard_map/reshape.17
  179.3 2.8 fusion.75
  182.1 1.6 fusion.66
  184.3 1.6 pad_maximum_fusion.1
  188.4 2.0 convolution_convert_fusion
  190.5 4.6 %pad_maximum_fusion = bf16[1536,3072]{1,0:T(8,128)(2,1)} fusion(bf16[1536,768]{1,0:T(8,128)(2,1)S(1)} %convolution_convert_fusion.1, bf16[1536,2304]{1,0:T(8,128)(2,1)S(1)} %convolution_convert_fusion), kind=kLoop, calls=%fused_computation.11 | loop fusion | flops 18874368 | bytes 18874368 | tf_op jit(solution)/shard_map/concatenate | solution.py:174
  195.1 5.5 %fusion.20 = bf16[128,1536]{1,0:T(8,128)(2,1)S(1)} fusion(bf16[128,2304]{1,0:T(8,128)(2,1)S(1)} %reshape.151, bf16[1536,3072]{1,0:T(8,128)(2,1)} %all-gather.2.cloned.1.call-done), kind=kOutput, calls=%fused_computation.30 | convolution fusion | flops 906166272 | bytes 8060928 | tf_op jit(solution)/shard_map/dot_general | solution.py:129
  201.1 2.9 convolution_convert_fusion.2
  204.1 1.4 collective-permute-start.2
  205.5 2.6 collective-permute-done.6
  208.8 3.5 %collective-permute-done.2 = bf16[1,2,8,8,1536]{4,2,1,3,0:T(8,128)(2,1)S(1)} collective-permute-done((bf16[1,2,8,8,1536]{4,2,1,3,0:T(8,128)(2,1)S(1)}, bf16[1,2,8,8,1536]{4,2,1,3,0:T(8,128)(2,1)S(1)}, u32[]{:S(2)}, u32[]{:S(2)}) %collective-permute-start.2) | collective-permute-done | bytes 393248 | tf_op jit(solution)/shard_map/ppermute | solution.py:13
  217.6 88.3 %reduce-scatter.2.cloned.1.call-done = bf16[96,3072]{1,0:T(8,128)(2,1)} async-done(((bf16[1536,3072]{1,0:T(8,128)(2,1)}), bf16[96,3072]{1,0:T(8,128)(2,1)}) %reduce-scatter.2.cloned.1.call-update) | async-done | bytes 589840 | tf_op jit(solution)/shard_map/reduce_scatter | solution.py:173
  305.9 2.2 convert_multiply_fusion
  (108 shorter events, 24.3 us)
Async XLA Ops:
  7.2 4.9 %copy-start.13 = (f32[1536]{0:T(1024)S(1)}, f32[1536]{0:T(1024)}, u32[]{:S(2)}) copy-start(f32[1536]{0:T(1024)} %param.12) | copy-start | bytes 18436
  7.2 5.3 %copy-start.19 = (s32[2,2]{1,0:T(2,128)S(1)}, s32[2,2]{1,0:T(2,128)}, u32[]{:S(2)}) copy-start(s32[2,2]{1,0:T(2,128)} %param.14) | copy-start | bytes 52
  7.2 90.9 %all-gather.2.cloned.1.call-start = ((), (), s32[]{:S(2)}) async-start(), calls=%async_computation.1 | async-start | bytes 10027008 | tf_op jit(solution)/shard_map/all_gather | solution.py:143
  7.9 298.0 %reduce-scatter.2.cloned.1.call-start = ((), (), s32[]{:S(2)}) async-start(), calls=%async_computation.2 | async-start | bytes 10027008 | tf_op jit(solution)/shard_map/reduce_scatter | solution.py:173
  9.0 4.6 %collective-permute-start.4 = (bf16[1,2,8,8,1536]{4,3,1,2,0:T(8,128)(2,1)S(1)}, bf16[1,2,8,8,1536]{4,3,1,2,0:T(8,128)(2,1)S(1)}, u32[]{:S(2)}, u32[]{:S(2)}) collective-permute-start(bf16[1,2,8,8,1536]{4,3,1,2,0:T(8,128)(2,1)S(1)} %bitcast.159), channel_id=1, source_target_pairs={{0,0},{1,1},{2,2},{3,3},{4,4},{5,5},{6,6},{7,7},{8,8},{9,9},{10,10... | collective-permute-start | bytes 1179656 | tf_op jit(solution)/shard_map/ppermute | solution.py:13
  12.4 1.9 collective-permute-start
  14.3 5.4 %collective-permute-start.5 = (bf16[1,2,8,8,1536]{4,3,2,1,0:T(8,128)(2,1)S(1)}, bf16[1,2,8,8,1536]{4,3,2,1,0:T(8,128)(2,1)S(1)}, u32[]{:S(2)}, u32[]{:S(2)}) collective-permute-start(bf16[1,2,8,8,1536]{4,3,2,1,0:T(8,128)(2,1)S(1)} %bitcast.161), channel_id=1, source_target_pairs={{0,15},{1,0},{2,1},{3,2},{4,3},{5,4},{6,5},{7,6},{8,7},{9,8},{10,9... | collective-permute-start | bytes 1179656 | tf_op jit(solution)/shard_map/ppermute | solution.py:13
  15.0 15.1 %collective-permute-start.1 = (bf16[1,2,8,8,1536]{4,3,2,1,0:T(8,128)(2,1)S(1)}, bf16[1,2,8,8,1536]{4,3,2,1,0:T(8,128)(2,1)S(1)}, u32[]{:S(2)}, u32[]{:S(2)}) collective-permute-start(bf16[1,2,8,8,1536]{4,3,2,1,0:T(8,128)(2,1)S(1)} %bitcast.163), channel_id=1, source_target_pairs={{0,15},{1,0},{2,1},{3,2},{4,3},{5,4},{6,5},{7,6},{8,7},{9,8},{10,9... | collective-permute-start | bytes 1179656 | tf_op jit(solution)/shard_map/ppermute | solution.py:13
  20.8 79.4 %copy-start.10 = (bf16[2,8,8,1536]{3,2,1,0:T(8,128)(2,1)}, bf16[2,8,8,1536]{3,2,1,0:T(8,128)(2,1)S(1)}, u32[]{:S(2)}) copy-start(bf16[2,8,8,1536]{3,2,1,0:T(8,128)(2,1)S(1)} %copy.60) | copy-start | bytes 1179652
  31.4 69.2 %copy-start.2 = (bf16[2,8,8,1536]{3,2,1,0:T(8,128)(2,1)}, bf16[2,8,8,1536]{3,2,1,0:T(8,128)(2,1)S(1)}, u32[]{:S(2)}) copy-start(bf16[2,8,8,1536]{3,2,1,0:T(8,128)(2,1)S(1)} %copy.42) | copy-start | bytes 1179652
  100.6 5.8 %copy-start = (bf16[2,8,8,12,64]{4,3,2,1,0:T(8,128)(2,1)}, bf16[2,8,8,12,64]{4,3,2,1,0:T(8,128)(2,1)S(1)}, u32[]{:S(2)}) copy-start(bf16[2,8,8,12,64]{4,3,2,1,0:T(8,128)(2,1)S(1)} %reshape.148) | copy-start | bytes 589828
  106.4 0.8 copy-start.5
  106.4 11.3 %copy-start.1 = (bf16[2,8,1,8,1,12,64]{6,5,4,3,1,0,2:T(8,128)(2,1)}, bf16[2,8,1,8,1,12,64]{6,5,4,3,1,0,2:T(8,128)(2,1)S(1)}, u32[]{:S(2)}) copy-start(bf16[2,8,1,8,1,12,64]{6,5,4,3,1,0,2:T(8,128)(2,1)S(1)} %get-tuple-element.21) | copy-start | bytes 589828
  106.4 11.3 %copy-start.7 = (bf16[2,8,1,8,1,12,64]{6,5,4,3,1,0,2:T(8,128)(2,1)}, bf16[2,8,1,8,1,12,64]{6,5,4,3,1,0,2:T(8,128)(2,1)S(1)}, u32[]{:S(2)}) copy-start(bf16[2,8,1,8,1,12,64]{6,5,4,3,1,0,2:T(8,128)(2,1)S(1)} %get-tuple-element.22) | copy-start | bytes 589828
  123.9 4.3 %copy-start.12 = (pred[2,64,64]{2,0,1:T(4,128)(4,1)S(1)}, pred[2,64,64]{2,0,1:T(4,128)(4,1)}, u32[]{:S(2)}) copy-start(pred[2,64,64]{2,0,1:T(4,128)(4,1)} %broadcast_compare_fusion) | copy-start | bytes 24580
  123.9 4.3 %copy-start.15 = (f32[2,225,12]{1,0,2:T(2,128)S(1)}, f32[2,225,12]{1,0,2:T(2,128)}, u32[]{:S(2)}) copy-start(f32[2,225,12]{1,0,2:T(2,128)} %param.16) | copy-start | bytes 64804
  123.9 4.3 %copy-start.16 = (s32[64,64]{1,0:T(8,128)S(1)}, s32[64,64]{1,0:T(8,128)}, u32[]{:S(2)}) copy-start(s32[64,64]{1,0:T(8,128)} %param.15) | copy-start | bytes 49156
  169.7 2.8 copy-start.8
  172.5 2.3 copy-start.4
  179.3 2.8 copy-start.6
  184.3 3.3 %copy-start.11 = (bf16[2,8,8,1536]{3,2,1,0:T(8,128)(2,1)S(1)}, bf16[2,8,8,1536]{3,2,1,0:T(8,128)(2,1)}, u32[]{:S(2)}) copy-start(bf16[2,8,8,1536]{3,2,1,0:T(8,128)(2,1)} %copy-done.10) | copy-start | bytes 1179652
  186.7 1.8 copy-start.3
  200.8 7.3 %copy-start.18 = (s32[2]{0:T(128)S(1)}, s32[2]{0:T(128)}, u32[]{:S(2)}) copy-start(s32[2]{0:T(128)} %get-tuple-element.17) | copy-start | bytes 28
  200.8 7.3 %collective-permute-start.6 = (bf16[1,2,8,8,1536]{4,2,1,3,0:T(8,128)(2,1)S(1)}, bf16[1,2,8,8,1536]{4,2,1,3,0:T(8,128)(2,1)S(1)}, u32[]{:S(2)}, u32[]{:S(2)}) collective-permute-start(bf16[1,2,8,8,1536]{4,2,1,3,0:T(8,128)(2,1)S(1)} %copy.71), channel_id=1, source_target_pairs={{0,1},{1,2},{2,3},{3,4},{4,5},{5,6},{6,7},{7,8},{8,9},{9,10},{10,1... | collective-permute-start | bytes 1179656 | tf_op jit(solution)/shard_map/ppermute | solution.py:13
  204.1 8.2 %collective-permute-start.2 = (bf16[1,2,8,8,1536]{4,2,1,3,0:T(8,128)(2,1)S(1)}, bf16[1,2,8,8,1536]{4,2,1,3,0:T(8,128)(2,1)S(1)}, u32[]{:S(2)}, u32[]{:S(2)}) collective-permute-start(bf16[1,2,8,8,1536]{4,2,1,3,0:T(8,128)(2,1)S(1)} %copy.53), channel_id=1, source_target_pairs={{0,1},{1,2},{2,3},{3,4},{4,5},{5,6},{6,7},{7,8},{8,9},{9,10},{10,1... | collective-permute-start | bytes 1179656 | tf_op jit(solution)/shard_map/ppermute | solution.py:13
  208.7 4.3 %collective-permute-start.7 = (bf16[1,2,8,8,1536]{4,2,3,1,0:T(8,128)(2,1)S(1)}, bf16[1,2,8,8,1536]{4,2,3,1,0:T(8,128)(2,1)S(1)}, u32[]{:S(2)}, u32[]{:S(2)}) collective-permute-start(bf16[1,2,8,8,1536]{4,2,3,1,0:T(8,128)(2,1)S(1)} %bitcast.165), channel_id=1, source_target_pairs={{0,0},{1,1},{2,2},{3,3},{4,4},{5,5},{6,6},{7,7},{8,8},{9,9},{10,10... | collective-permute-start | bytes 1179656 | tf_op jit(solution)/shard_map/ppermute | solution.py:13
  212.9 1.2 copy-start.17
  212.9 0.6 collective-permute-start.3
  213.1 2.2 copy-start.14
  213.5 2.1 copy-start.9
Sparse Core Ops, SparseCore 0:
  10.3 87.7 all-gather.1
  195.2 110.6 reduce-scatter.1
where the time goes:
time: 317 us; the launch traced here: 315 us
  waiting for transfers between devices  174 us (55%)
  other arithmetic  47.9 us (15%)
  local copies, waits for them, and re-layouts  40.4 us (13%)
  matrix products  35 us (11%)
  between operations  14.8 us (5%)
    reduce_scatter x1, waiting for transfers between devices, on_device(): lax.psum_scatter(jnp.concatenate([first, second], axis=1).astype(jnp.bflo...  88.3 us
    all_gather x1, waiting for transfers between devices, on_device(): full_weights = lax.all_gather(weights, 'lon', axis=0, tiled=True)  66.7 us
    sub x1, other arithmetic, attend_forward(): expo = jnp.exp(scores - top)  21.7 us
    ppermute x8, waiting for transfers between devices, passed_along(): lax.ppermute(shard, axis, [(i, (i + by) % count) for i in range(count)])  18.6 us
    sub x1, other arithmetic, attend_backward(): grad_probs - jnp.sum(probs * grad_probs, axis=-1, keepdims=True)  11.2 us
    mul x2, local copies, waits for them, and re-layouts, attend_forward(): scores.reshape(levels, windows, heads, area, area) * scale  8.12 us
    reshape x2, local copies, waits for them, and re-layouts, attend_backward(): grad_probs = grad_probs.reshape(probs.shape)  8.11 us
    another operation x3, local copies, waits for them, and re-layouts  7.23 us
  transfers between devices with their start and end apart: 10, of which 6 were waited for; matrix products, arithmetic and copies ran while one was open for 8% of the time, Pallas kernels for 0%

commit v1 on v0

v1 whole, which is shorter than its diff:
```python
import functools
import math

import jax
import jax.numpy as jnp
from jax import lax
from jax.experimental import pallas as pl
from jax.experimental.pallas import tpu as pltpu
from jax.sharding import Mesh
from jax.sharding import PartitionSpec as P

epsilon = 1e-05
LON = ("chip", "core")


def along_lon(shard, by):
    chips, cores = lax.axis_size("chip"), lax.axis_size("core")
    count = chips * cores
    return lax.ppermute(shard, LON, [(i, (i + by) % count) for i in range(count)])


def along_lat(shard, by):
    count = lax.axis_size("lat")
    return lax.ppermute(shard, "lat", [(i, (i + by) % count) for i in range(count)])


def swap_cores(shard):
    return lax.ppermute(shard, "core", [(0, 1), (1, 0)])


def pick(rows, cols, levels, side, over_rows):
    tile = levels * side * side
    shape = (tile, 2 * tile)
    target = lax.broadcasted_iota(jnp.int32, shape, 0)
    source = lax.broadcasted_iota(jnp.int32, shape, 1)
    level = target // (side * side)
    row = target // side % side
    col = target % side
    from_row = jnp.full_like(row, rows[levels - 1])
    from_col = jnp.full_like(col, cols[levels - 1])
    for l in range(levels - 1):
        from_row = jnp.where(level == l, rows[l], from_row)
        from_col = jnp.where(level == l, cols[l], from_col)
    from_row = row + from_row
    from_col = col + from_col
    which = (from_row if over_rows else from_col) // side
    wanted = which * tile + level * side * side + from_row % side * side + from_col % side
    return (source == wanted).astype(jnp.bfloat16)


def picked(onehot, first, second):
    both = jnp.concatenate([first, second], axis=0)
    return jnp.dot(onehot, both, preferred_element_type=jnp.float32).astype(jnp.bfloat16)


def roll_forward(field, shifts, levels, side):
    zeros = jnp.zeros_like(shifts[:, 0])
    rows = shifts[:, 0]
    if lax.axis_size("lat") > 1:
        field = picked(pick(rows, zeros, levels, side, True), field, along_lat(field, -1))
        rows = zeros
    return picked(pick(rows, shifts[:, 1], levels, side, False), field, along_lon(field, -1))


def roll_back(field, shifts, levels, side):
    zeros = jnp.zeros_like(shifts[:, 0])
    rows = side - shifts[:, 0]
    more = lax.axis_size("lat") > 1
    field = picked(
        pick(zeros if more else rows, side - shifts[:, 1], levels, side, False),
        along_lon(field, 1),
        field,
    )
    if more:
        field = picked(pick(rows, zeros, levels, side, True), along_lat(field, 1), field)
    return field


def middle_kernel(area, head, own_ref, other_ref, turned_ref, w_ref, bias_ref, gw_ref, mixed_ref, grad_ref, qkv_ref, gm_ref):
    tile, both = own_ref.shape
    width = both // 2
    part = w_ref.shape[1] // 4
    levels, pairs = bias_ref.shape[:2]
    scale = 1.0 / math.sqrt(head)
    for t, x_ref in enumerate((own_ref, other_ref)):
        rows = pl.ds(t * tile, tile)
        for n in range(3):
            cols = pl.ds(n * part, part)
            qkv_ref[rows, cols] = jnp.dot(
                x_ref[:, :width], w_ref[:, cols], preferred_element_type=jnp.float32
            ).astype(jnp.bfloat16)
        gm_ref[rows, :] = jnp.dot(
            x_ref[:, width:], w_ref[:, 3 * part :], preferred_element_type=jnp.float32
        ).astype(jnp.bfloat16)
    lane = lax.broadcasted_iota(jnp.int32, (area, 2 * head), 1)
    left = lane < head

    def stacked(pair):
        zero = jnp.zeros_like(pair)
        return jnp.concatenate([jnp.where(left, pair, zero), jnp.where(left, zero, pair)], axis=0)

    def unstacked(product):
        return jnp.where(left, product[:area], product[area:]).astype(jnp.bfloat16)

    def across(a, b):
        return lax.dot_general(a, b, (((1,), (1,)), ((), ())), preferred_element_type=jnp.float32)

    def down(a, b):
        return lax.dot_general(a, b, (((0,), (0,)), ((), ())), preferred_element_type=jnp.float32)

    for w in range(2 * tile // area):
        rows = pl.ds(w * area, area)
        for p in range(pairs):
            at = p * 2 * head
            q_cols, k_cols, v_cols = (pl.ds(n * part + at, 2 * head) for n in range(3))
            query = stacked(qkv_ref[rows, q_cols])
            keys = qkv_ref[rows, k_cols]
            values = qkv_ref[rows, v_cols]
            upstream = stacked(gm_ref[rows, q_cols])
            scores = across(query, keys) * scale + bias_ref[w % levels, p]
            expo = jnp.exp(scores - jnp.max(scores, axis=-1, keepdims=True))
            probs = expo / jnp.sum(expo, axis=-1, keepdims=True)
            probs_b = probs.astype(jnp.bfloat16)
            mixed_ref[rows, q_cols] = unstacked(
                jnp.dot(probs_b, values, preferred_element_type=jnp.float32)
            )
            grad_probs = across(upstream, values)
            grad_ref[rows, v_cols] = down(probs_b, upstream).astype(jnp.bfloat16)
            inner = jnp.sum(probs * grad_probs, axis=-1, keepdims=True)
            grad_scores = (probs * (grad_probs - inner) * scale).astype(jnp.bfloat16)
            grad_ref[rows, q_cols] = unstacked(
                jnp.dot(grad_scores, keys, preferred_element_type=jnp.float32)
            )
            grad_ref[rows, k_cols] = down(grad_scores, query).astype(jnp.bfloat16)
    for m in range(2):
        rows = pl.ds(m * (width // 2), width // 2)
        for n in range(3):
            cols = pl.ds(n * part, part)
            gw_ref[rows, cols] = jnp.dot(
                turned_ref[rows, :], grad_ref[:, cols], preferred_element_type=jnp.float32
            ).astype(jnp.bfloat16)
        lower = pl.ds(width + m * (width // 2), width // 2)
        gw_ref[rows, 3 * part :] = jnp.dot(
            turned_ref[lower, :], mixed_ref[...], preferred_element_type=jnp.float32
        ).astype(jnp.bfloat16)


def outer_kernel(mixed_ref, grad_ref, w_ref, own_ref, other_ref):
    tile = own_ref.shape[0]
    width = w_ref.shape[0]
    part = w_ref.shape[1] // 4
    step = width // 4
    for n in range(4):
        rows = pl.ds(n * step, step)
        for k, (x_ref, w_cols) in enumerate(((mixed_ref, pl.ds(3 * part, part)), (grad_ref, pl.ds(0, 3 * part)))):
            product = lax.dot_general(
                x_ref[...], w_ref[rows, w_cols], (((1,), (1,)), ((), ())), preferred_element_type=jnp.float32
            )
            cols = pl.ds(k * width + n * step, step)
            own_ref[:, cols] = product[:tile]
            other_ref[:, cols] = product[tile:].astype(jnp.bfloat16)


def on_device(tokens, land, surface, gain, weights, shifts, index_table, bias_table, cotangent):
    levels, side, _, width = tokens.shape
    area = side * side
    tile = levels * area
    heads = bias_table.shape[2]
    entries = bias_table.shape[1]
    own_rows = weights.shape[0]
    cores = lax.axis_size("core")
    part = weights.shape[1] // 4 // cores
    head = weights.shape[1] // 4 // heads
    own_heads = heads // cores
    core = lax.axis_index("core")
    first_core = core == 0

    halves = weights.reshape(own_rows, 4, cores, part)
    low = halves[:, :, 0].reshape(own_rows, 4 * part)
    high = halves[:, :, 1].reshape(own_rows, 4 * part)
    kept = jnp.where(first_core, low, high)
    came = swap_cores(jnp.where(first_core, high, low))
    chip_rows = jnp.concatenate(
        [jnp.where(first_core, kept, came), jnp.where(first_core, came, kept)], axis=0
    )
    w_own = lax.all_gather(chip_rows, "chip", axis=0, tiled=True)

    surface_term = jnp.where(land[None, :, :, None] == 1, surface[1], surface[0])
    stream = (tokens.astype(jnp.float32) + surface_term).astype(jnp.bfloat16).reshape(tile, width)
    flat_cot = cotangent.reshape(tile, width)
    values = stream.astype(jnp.float32)
    center = values - jnp.mean(values, axis=-1, keepdims=True)
    spread = lax.rsqrt(jnp.mean(center * center, axis=-1, keepdims=True) + epsilon)
    normed = (center * spread * gain).astype(jnp.bfloat16)
    own = roll_forward(jnp.concatenate([normed, flat_cot], axis=1), shifts, levels, side)
    other = swap_cores(own)
    turned = jnp.concatenate([own.T, other.T], axis=1)

    onehot = (index_table[:, :, None] == jnp.arange(entries, dtype=jnp.int32)).astype(jnp.float32)
    own_table = lax.dynamic_slice_in_dim(bias_table, core * own_heads, own_heads, 2)
    bias = jnp.einsum("qkr,lrh->lhqk", onehot, own_table, precision=lax.Precision.HIGHEST)
    row_number = lax.axis_index("lat") * side + jnp.arange(side, dtype=jnp.int32)
    group = row_number[None, :] >= (side * lax.axis_size("lat") - shifts[:, 0])[:, None]
    group = jnp.repeat(group, side, axis=1)
    allowed = group[:, :, None] == group[:, None, :]
    bias = jnp.where(allowed[:, None], bias, -1e30).reshape(levels, own_heads // 2, 2 * area, area)

    grad_tile, mixed, grad_qkv = pl.pallas_call(
        functools.partial(middle_kernel, area, head),
        out_shape=(
            jax.ShapeDtypeStruct((width, 4 * part), jnp.bfloat16),
            jax.ShapeDtypeStruct((2 * tile, part), jnp.bfloat16),
            jax.ShapeDtypeStruct((2 * tile, 3 * part), jnp.bfloat16),
        ),
        scratch_shapes=[
            pltpu.VMEM((2 * tile, 3 * part), jnp.bfloat16),
            pltpu.VMEM((2 * tile, part), jnp.bfloat16),
        ],
        compiler_params=pltpu.CompilerParams(vmem_limit_bytes=40 * 1024 * 1024),
        cost_estimate=pl.CostEstimate(
            flops=2 * 2 * 2 * tile * width * 4 * part, bytes_accessed=12_000_000, transcendentals=0
        ),
        name="attention",
    )(own, other, turned, w_own, bias)

    summed = lax.psum_scatter(grad_tile, "chip", scatter_dimension=0, tiled=True)

    attended_own, attended_other = pl.pallas_call(
        outer_kernel,
        out_shape=(
            jax.ShapeDtypeStruct((tile, 2 * width), jnp.float32),
            jax.ShapeDtypeStruct((tile, 2 * width), jnp.bfloat16),
        ),
        compiler_params=pltpu.CompilerParams(vmem_limit_bytes=40 * 1024 * 1024),
        cost_estimate=pl.CostEstimate(
            flops=2 * 2 * tile * width * 4 * part, bytes_accessed=8_000_000, transcendentals=0
        ),
        name="projections",
    )(mixed, grad_qkv, w_own)
    back = (attended_own + swap_cores(attended_other).astype(jnp.float32)).astype(jnp.bfloat16)
    back = roll_back(back, shifts, levels, side)
    output = (values + back[:, :width].astype(jnp.float32)).astype(jnp.bfloat16)
    scaled = center * spread
    upstream = back[:, width:].astype(jnp.float32) * gain
    grad_stream = spread * (
        upstream
        - jnp.mean(upstream, axis=-1, keepdims=True)
        - scaled * jnp.mean(upstream * scaled, axis=-1, keepdims=True)
    )
    grad_tokens = (flat_cot.astype(jnp.float32) + grad_stream).astype(jnp.bfloat16)

    summed = lax.psum(summed, "lat") if lax.axis_size("lat") > 1 else summed
    top, bottom = summed[:own_rows], summed[own_rows:]
    mine = jnp.where(first_core, top, bottom)
    theirs = swap_cores(jnp.where(first_core, bottom, top))
    token_count = tile * lax.axis_size("lat") * lax.axis_size("chip") * cores
    both = jnp.stack(
        [
            jnp.where(first_core, mine, theirs).reshape(own_rows, 4, part),
            jnp.where(first_core, theirs, mine).reshape(own_rows, 4, part),
        ],
        axis=2,
    )
    grad_weights = both.reshape(own_rows, -1).astype(jnp.float32) * (1.0 / math.sqrt(token_count))
    return (output.reshape(tokens.shape), grad_tokens.reshape(tokens.shape), grad_weights)


def solution(mesh):
    sizes = dict(mesh.shape)
    devices = mesh.devices.reshape(sizes["grp"], sizes["lon"] // 2, 2, sizes["lat"])
    finer = Mesh(devices, ("grp", "chip", "core", "lat"))
    return jax.shard_map(
        on_device,
        mesh=finer,
        in_specs=(
            P("grp", "lat", LON, None),
            P(("grp", "lat"), LON),
            P(),
            P(),
            P(LON, None),
            P(),
            P(),
            P("lat", None, None),
            P("grp", "lat", LON, None),
        ),
        out_specs=(
            P("grp", "lat", LON, None),
            P("grp", "lat", LON, None),
            P(("grp",) + LON, None),
        ),
        check_vma=False,
    )
```

time: 317 us -> 232 us (0.73)
  other arithmetic: 47.9 us -> 7.1 us
  matrix products: 35 us -> 9.38 us
  local copies, waits for them, and re-layouts: 40.4 us -> 19.6 us
  waiting for transfers between devices: 174 us -> 158 us
  Pallas kernels: 0 us -> 12.2 us
  starting transfers between devices: 2.55 us -> 8.37 us
    sub x2, other arithmetic: 32.9 us -> 0.12 us  [the longest x1 0.11 us: roll_back(): side - shifts[:, 1]]
    dot_general x13 -> x3, matrix products: 35 us -> 9.38 us  [the longest x2 6.73 us: picked(): jnp.dot(onehot, both, preferred_element_type=jnp.float32)]
    all_gather x1, waiting for transfers between devices: 66.7 us -> 53.5 us  [on_device(): w_own = lax.all_gather(chip_rows, 'chip', axis=0, tiled=True)]
    pallas_call x0 -> x2, Pallas kernels: none -> 12.2 us  [the longest x1 10.2 us: on_device(): pl.pallas_call(functools.partial(middle_kernel, area, head), out_shape=(j...]
    reduce_scatter x1, waiting for transfers between devices: 88.3 us -> 77.2 us  [on_device(): lax.psum_scatter(grad_tile, 'chip', scatter_dimension=0, tiled=True)]
    ppermute x8 -> x6, waiting for transfers between devices: 18.6 us -> 27.8 us  [the longest x2 23.8 us: along_lon(): lax.ppermute(shard, LON, [(i, (i + by) % count) for i in range(count)])]
    reshape x5 -> x1, local copies, waits for them, and re-layouts: 10.5 us -> 2.21 us  [on_device(): halves = weights.reshape(own_rows, 4, cores, part)]
    another operation x6 -> x4, local copies, waits for them, and re-layouts: 8.28 us -> 0.22 us  [on_device(): jnp.stack([jnp.where(first_core, mine, theirs).reshape(own_rows, 4, part)...]
  transfers between devices with their start and end apart: 10 -> 8, of which waited for: 6 -> 7; matrix products, arithmetic and copies ran while one was open for 8% -> 7% of each run, Pallas kernels for 0% -> 1%
where the time goes in v1:
time: 232 us; the launch traced here: 230 us
  waiting for transfers between devices  158 us (68%)
  local copies, waits for them, and re-layouts  19.6 us (8%)
  between operations  14.5 us (6%)
  Pallas kernels  12.2 us (5%)
  matrix products  9.38 us (4%)
  starting transfers between devices  8.37 us (4%)
  other arithmetic  7.1 us (3%)
    reduce_scatter x1, waiting for transfers between devices, on_device(): lax.psum_scatter(grad_tile, 'chip', scatter_dimension=0, tiled=True)  77.2 us
    all_gather x1, waiting for transfers between devices, on_device(): w_own = lax.all_gather(chip_rows, 'chip', axis=0, tiled=True)  53.5 us
    ppermute x2, waiting for transfers between devices, along_lon(): lax.ppermute(shard, LON, [(i, (i + by) % count) for i in range(count)])  23.8 us
    unnamed x42, local copies, waits for them, and re-layouts  10.4 us
    pallas_call x1, Pallas kernels, on_device(): pl.pallas_call(functools.partial(middle_kernel, area, head), out_shape=(j...  10.2 us
    ppermute x4, starting transfers between devices, swap_cores(): return lax.ppermute(shard, 'core', [(0, 1), (1, 0)])  7.62 us
    dot_general x2, matrix products, picked(): jnp.dot(onehot, both, preferred_element_type=jnp.float32)  6.73 us
  transfers between devices with their start and end apart: 8, of which 7 were waited for; matrix products, arithmetic and copies ran while one was open for 7% of the time, Pallas kernels for 1%

profile of v1, /device:TPU:6, one launch (start us, length us, event | category | flops | bytes accessed | tf_op | source)
XLA Modules:
  0.0 229.6 jit_solution(7092559038060402420)
XLA Ops:
  7.2 2.2 reshape.105
  9.4 0.8 fusion.141
  10.3 0.3 broadcast_select_fusion.1
  10.8 1.5 collective-permute-done.2
  12.3 0.9 pad_maximum_fusion.2
  14.5 0.5 collective-permute-start
  15.0 0.7 fusion.144
  15.8 10.6 %collective-permute-done = bf16[128,3072]{1,0:T(8,128)(2,1)S(1)} collective-permute-done((bf16[128,3072]{1,0:T(8,128)(2,1)S(1)}, bf16[128,3072]{1,0:T(8,128)(2,1)S(1)}, u32[]{:S(2)}, u32[]{:S(2)}) %collective-permute-start) | collective-permute-done | bytes 786464 | tf_op jit(solution)/shard_map/ppermute | solution.py:19
  26.4 3.6 %convolution_convert_fusion.1 = bf16[128,3072]{0,1:T(8,128)(2,1)S(1)} fusion(bf16[128,3072]{1,0:T(8,128)(2,1)S(1)} %collective-permute-done, bf16[128,1536]{1,0:T(8,128)(2,1)S(1)} %bitcast.62, bf16[128,1536]{1,0:T(8,128)(2,1)S(1)} %fusion.21, s32[]{:T(128)} %bitcast.8, s32[]{:T(128)} %bitcast.7, s32[]{:T(128)} %bitcast.6, s32[]{:T(128)} %bitcast.5, ...), kind=kOutput, calls=%fused_computation.4 | convolution fusion | flops 208273408 | bytes 2362768 | tf_op jit(solution)/shard_map/dot_general | solution.py:53
  30.0 7.2 %collective-permute-start.1 = (bf16[128,3072]{0,1:T(8,128)(2,1)S(1)}, bf16[128,3072]{0,1:T(8,128)(2,1)S(1)}, u32[]{:S(2)}, u32[]{:S(2)}) collective-permute-start(bf16[128,3072]{0,1:T(8,128)(2,1)S(1)} %convolution_convert_fusion.1), channel_id=1, source_target_pairs={{0,1},{1,0},{2,3},{3,2},{4,5},{5,4},{6,7},{7,6},{8,9},{9,8},{10,11... | collective-permute-start | bytes 2359304 | tf_op jit(solution)/shard_map/ppermute | solution.py:28
  37.6 2.7 %fusion.12 = f32[2,6,64,64]{3,1,2,0:T(8,128)S(1)} fusion(s32[64,64]{1,0:T(8,128)S(1)} %copy-done.19, pred[2,64,64]{2,1,0:T(8,128)(4,1)S(1)} %broadcast_compare_fusion, f32[2,225,6]{1,0,2:T(2,128)S(1)} %constant_dynamic-slice_fusion), kind=kOutput, calls=%fused_computation.16 | convolution fusion | flops 133681152 | bytes 231984 | tf_op jit(solution)/shard_map/qkr,lrh->lhqk/dot_general | solution.py:201
  40.2 0.8 copy.33
  41.7 0.6 copy-done.10
  42.3 1.5 pad_maximum_fusion.turned_ref
  43.8 53.5 %all-gather.2.cloned.1.call-done.w_ref = bf16[1536,1536]{1,0:T(8,128)(2,1)} async-done(((bf16[192,1536]{1,0:T(8,128)(2,1)}), bf16[1536,1536]{1,0:T(8,128)(2,1)}) %all-gather.2.cloned.1.call-update) | async-done | bytes 4718608 | tf_op jit(solution)/shard_map/all_gather | solution.py:186
  97.3 2.3 %copy-done.2 = bf16[1536,1536]{1,0:T(8,128)(2,1)S(1)} copy-done((bf16[1536,1536]{1,0:T(8,128)(2,1)S(1)}, bf16[1536,1536]{1,0:T(8,128)(2,1)}, u32[]{:S(2)}) %copy-start.2) | copy-done | bytes 4718616
  99.6 1.0 copy-done.6
  100.6 10.2 %attention.1 = (bf16[1536,1536]{1,0:T(8,128)(2,1)S(1)}, bf16[256,384]{1,0:T(8,128)(2,1)S(1)}, bf16[256,1152]{1,0:T(8,128)(2,1)S(1)}) custom-call(bf16[128,3072]{1,0:T(8,128)(2,1)S(1)} %copy.34.own_ref, bf16[128,3072]{1,0:T(8,128)(2,1)S(1)} %copy.35.other_ref, bf16[3072,256]{1,0:T(8,128)(2,1)S(1)} %pad_maximum_fusion.turned_ref, ...), custom_call_target="tpu_custom_call" | custom-call | flops 2415919104 | bytes 12000000 | tf_op jit(solution)/shard_map/attention/pallas_call | solution.py:208
  110.8 2.2 copy-done.1
  113.0 0.8 copy-done.4
  113.8 1.0 copy-done.5
  114.9 2.3 %copy-done.3 = bf16[1536,1536]{1,0:T(8,128)(2,1)S(1)} copy-done((bf16[1536,1536]{1,0:T(8,128)(2,1)S(1)}, bf16[1536,1536]{1,0:T(8,128)(2,1)}, u32[]{:S(2)}) %copy-start.3) | copy-done | bytes 4718616
  117.2 2.0 projections.1
  119.5 2.3 collective-permute-done.3
  122.2 0.6 fusion.142
  122.8 13.2 %collective-permute-done.4 = bf16[128,3072]{1,0:T(8,128)(2,1)S(1)} collective-permute-done((bf16[128,3072]{1,0:T(8,128)(2,1)S(1)}, bf16[128,3072]{1,0:T(8,128)(2,1)S(1)}, u32[]{:S(2)}, u32[]{:S(2)}) %collective-permute-start.4) | collective-permute-done | bytes 786464 | tf_op jit(solution)/shard_map/ppermute | solution.py:19
  136.0 3.1 %convolution_convert_fusion = bf16[128,3072]{1,0:T(8,128)(2,1)S(1)} fusion(bf16[128,3072]{1,0:T(8,128)(2,1)S(1)} %add_convert_fusion, bf16[128,3072]{1,0:T(8,128)(2,1)S(1)} %collective-permute-done.4, s32[]{:T(128)} %bitcast.4, s32[]{:T(128)} %bitcast.3, s32[128]{0:T(128)S(1)} %get-tuple-element.43, s32[128]{0:T(128)S(1)} %get-tuple-element.45, s32[]{:T(128)} %bitcast.2, ...), kind=kOutput, calls=%fused_computation.3 | convolution fusion | flops 206700544 | bytes 2362768 | tf_op jit(solution)/shard_map/dot_general | solution.py:53
  139.5 77.2 %reduce-scatter.2.cloned.1.call-done = bf16[192,1536]{1,0:T(8,128)(2,1)} async-done(((bf16[1536,1536]{1,0:T(8,128)(2,1)}), bf16[192,1536]{1,0:T(8,128)(2,1)}) %reduce-scatter.2.cloned.1.call-update) | async-done | bytes 589840 | tf_op jit(solution)/shard_map/reduce_scatter | solution.py:226
  216.7 1.1 broadcast_select_fusion.4
  217.9 1.4 fusion.26
  219.9 0.9 copy.38
  220.8 2.0 mul.101
  (80 shorter events, 4.2 us)
Async XLA Ops:
  7.2 30.3 %copy-start = (f32[2,225,12]{1,0,2:T(2,128)S(1)}, f32[2,225,12]{1,0,2:T(2,128)}, u32[]{:S(2)}) copy-start(f32[2,225,12]{1,0,2:T(2,128)} %param.16) | copy-start | bytes 64804
  7.2 90.1 %all-gather.2.cloned.1.call-start = ((), (), s32[]{:S(2)}) async-start(), calls=%async_computation.1 | async-start | bytes 5308416 | tf_op jit(solution)/shard_map/all_gather | solution.py:186
  10.6 1.6 collective-permute-start.2
  10.8 2.5 %copy-start.17 = (f32[2,1536]{1,0:T(2,128)S(1)}, f32[2,1536]{1,0:T(2,128)}, u32[]{:S(2)}) copy-start(f32[2,1536]{1,0:T(2,128)} %param.11) | copy-start | bytes 36868
  10.8 2.6 %copy-start.18 = (s32[8,8]{1,0:T(8,128)S(1)}, s32[8,8]{1,0:T(8,128)}, u32[]{:S(2)}) copy-start(s32[8,8]{1,0:T(8,128)} %param.10) | copy-start | bytes 772
  12.3 1.2 copy-start.14
  13.2 0.9 copy-start.15
  13.2 1.2 copy-start.12
  13.2 203.4 %reduce-scatter.2.cloned.1.call-start = ((), (), s32[]{:S(2)}) async-start(), calls=%async_computation.2 | async-start | bytes 5308416 | tf_op jit(solution)/shard_map/reduce_scatter | solution.py:226
  13.6 16.4 %copy-start.7 = (bf16[2,8,8,1536]{3,2,1,0:T(8,128)(2,1)}, bf16[2,8,8,1536]{3,2,1,0:T(8,128)(2,1)S(1)}, u32[]{:S(2)}) copy-start(bf16[2,8,8,1536]{3,2,1,0:T(8,128)(2,1)S(1)} %get-tuple-element.18) | copy-start | bytes 1179652
  13.6 1.4 copy-start.16
  14.5 11.9 %collective-permute-start = (bf16[128,3072]{1,0:T(8,128)(2,1)S(1)}, bf16[128,3072]{1,0:T(8,128)(2,1)S(1)}, u32[]{:S(2)}, u32[]{:S(2)}) collective-permute-start(bf16[128,3072]{1,0:T(8,128)(2,1)S(1)} %pad_maximum_fusion.1), channel_id=1, source_target_pairs={{0,15},{1,0},{2,1},{3,2},{4,3},{5,4},{6,5},{7,6},{8,7},{9,8},{10,9... | collective-permute-start | bytes 2359304 | tf_op jit(solution)/shard_map/ppermute | solution.py:19
  26.4 11.2 %copy-start.19 = (s32[64,64]{1,0:T(8,128)S(1)}, s32[64,64]{1,0:T(8,128)}, u32[]{:S(2)}) copy-start(s32[64,64]{1,0:T(8,128)} %param.15) | copy-start | bytes 49156
  30.0 11.3 %copy-start.9 = (bf16[128,3072]{0,1:T(8,128)(2,1)}, bf16[128,3072]{0,1:T(8,128)(2,1)S(1)}, u32[]{:S(2)}) copy-start(bf16[128,3072]{0,1:T(8,128)(2,1)S(1)} %convolution_convert_fusion.1) | copy-start | bytes 2359300
  30.0 11.3 %collective-permute-start.1 = (bf16[128,3072]{0,1:T(8,128)(2,1)S(1)}, bf16[128,3072]{0,1:T(8,128)(2,1)S(1)}, u32[]{:S(2)}, u32[]{:S(2)}) collective-permute-start(bf16[128,3072]{0,1:T(8,128)(2,1)S(1)} %convolution_convert_fusion.1), channel_id=1, source_target_pairs={{0,1},{1,0},{2,3},{3,2},{4,5},{5,4},{6,7},{7,6},{8,9},{9,8},{10,11... | collective-permute-start | bytes 2359304 | tf_op jit(solution)/shard_map/ppermute | solution.py:28
  41.4 0.9 copy-start.10
  97.3 2.3 %copy-start.2 = (bf16[1536,1536]{1,0:T(8,128)(2,1)S(1)}, bf16[1536,1536]{1,0:T(8,128)(2,1)}, u32[]{:S(2)}) copy-start(bf16[1536,1536]{1,0:T(8,128)(2,1)} %all-gather.2.cloned.1.call-done.w_ref) | copy-start | bytes 14155780
  99.6 1.0 copy-start.6
  110.8 2.2 copy-start.1
  113.0 0.8 copy-start.4
  113.8 1.1 copy-start.5
  114.9 2.3 %copy-start.3 = (bf16[1536,1536]{1,0:T(8,128)(2,1)S(1)}, bf16[1536,1536]{1,0:T(8,128)(2,1)}, u32[]{:S(2)}) copy-start(bf16[1536,1536]{1,0:T(8,128)(2,1)} %all-gather.2.cloned.1.call-done.w_ref) | copy-start | bytes 14155780
  119.2 2.6 %collective-permute-start.3 = (bf16[128,3072]{1,0:T(8,128)(2,1)S(1)}, bf16[128,3072]{1,0:T(8,128)(2,1)S(1)}, u32[]{:S(2)}, u32[]{:S(2)}) collective-permute-start(bf16[128,3072]{1,0:T(8,128)(2,1)S(1)} %get-tuple-element.11), channel_id=1, source_target_pairs={{0,1},{1,0},{2,3},{3,2},{4,5},{5,4},{6,7},{7,6},{8,9},{9,8},{10,11... | collective-permute-start | bytes 2359304 | tf_op jit(solution)/shard_map/ppermute | solution.py:28
  122.0 14.0 %collective-permute-start.4 = (bf16[128,3072]{1,0:T(8,128)(2,1)S(1)}, bf16[128,3072]{1,0:T(8,128)(2,1)S(1)}, u32[]{:S(2)}, u32[]{:S(2)}) collective-permute-start(bf16[128,3072]{1,0:T(8,128)(2,1)S(1)} %add_convert_fusion), channel_id=1, source_target_pairs={{0,1},{1,2},{2,3},{3,4},{4,5},{5,6},{6,7},{7,8},{8,9},{9,10},{10,1... | collective-permute-start | bytes 2359304 | tf_op jit(solution)/shard_map/ppermute | solution.py:19
  136.0 3.2 %copy-start.8 = (bf16[2,8,8,1536]{3,2,1,0:T(8,128)(2,1)S(1)}, bf16[2,8,8,1536]{3,2,1,0:T(8,128)(2,1)}, u32[]{:S(2)}) copy-start(bf16[2,8,8,1536]{3,2,1,0:T(8,128)(2,1)} %copy-done.7) | copy-start | bytes 1179652
  139.2 78.7 %copy-start.13 = (bf16[2,8,8,1536]{3,2,1,0:T(8,128)(2,1)S(1)}, bf16[2,8,8,1536]{3,2,1,0:T(8,128)(2,1)}, u32[]{:S(2)}) copy-start(bf16[2,8,8,1536]{3,2,1,0:T(8,128)(2,1)} %param.17) | copy-start | bytes 1179652
  216.7 2.8 %copy-start.11 = (bf16[192,1536]{1,0:T(8,128)(2,1)S(1)}, bf16[192,1536]{1,0:T(8,128)(2,1)}, u32[]{:S(2)}) copy-start(bf16[192,1536]{1,0:T(8,128)(2,1)} %reduce-scatter.2.cloned.1.call-done) | copy-start | bytes 1769476
  217.8 1.6 collective-permute-start.5
Sparse Core Ops, SparseCore 0:
  13.3 83.8 all-gather.1
  113.9 102.6 reduce-scatter.1

commit v2 on v1

v2 whole, which is shorter than its diff:
```python
import functools
import math

import jax
import jax.numpy as jnp
from jax import lax
from jax.experimental import pallas as pl
from jax.experimental.pallas import tpu as pltpu
from jax.sharding import Mesh
from jax.sharding import PartitionSpec as P

epsilon = 1e-05
LON = ("far", "near", "side", "core")


def along_lon(shard, by):
    count = math.prod(lax.axis_size(axis) for axis in LON)
    return lax.ppermute(shard, LON, [(i, (i + by) % count) for i in range(count)])


def along_lat(shard, by):
    count = lax.axis_size("lat")
    return lax.ppermute(shard, "lat", [(i, (i + by) % count) for i in range(count)])


def swap(shard, axis):
    return lax.ppermute(shard, axis, [(0, 1), (1, 0)])


def pick(rows, cols, levels, side, over_rows):
    tile = levels * side * side
    shape = (tile, 2 * tile)
    target = lax.broadcasted_iota(jnp.int32, shape, 0)
    source = lax.broadcasted_iota(jnp.int32, shape, 1)
    level = target // (side * side)
    row = target // side % side
    col = target % side
    from_row = jnp.full_like(row, rows[levels - 1])
    from_col = jnp.full_like(col, cols[levels - 1])
    for l in range(levels - 1):
        from_row = jnp.where(level == l, rows[l], from_row)
        from_col = jnp.where(level == l, cols[l], from_col)
    from_row = row + from_row
    from_col = col + from_col
    which = (from_row if over_rows else from_col) // side
    wanted = which * tile + level * side * side + from_row % side * side + from_col % side
    return (source == wanted).astype(jnp.bfloat16)


def picked(onehot, first, second):
    both = jnp.concatenate([first, second], axis=0)
    return jnp.dot(onehot, both, preferred_element_type=jnp.float32).astype(jnp.bfloat16)


def roll_forward(field, shifts, levels, side):
    zeros = jnp.zeros_like(shifts[:, 0])
    rows = shifts[:, 0]
    if lax.axis_size("lat") > 1:
        field = picked(pick(rows, zeros, levels, side, True), field, along_lat(field, -1))
        rows = zeros
    return picked(pick(rows, shifts[:, 1], levels, side, False), field, along_lon(field, -1))


def roll_back(field, shifts, levels, side):
    zeros = jnp.zeros_like(shifts[:, 0])
    rows = side - shifts[:, 0]
    more = lax.axis_size("lat") > 1
    field = picked(
        pick(zeros if more else rows, side - shifts[:, 1], levels, side, False),
        along_lon(field, 1),
        field,
    )
    if more:
        field = picked(pick(rows, zeros, levels, side, True), along_lat(field, 1), field)
    return field


def attention_kernel(area, head, pieces, *refs):
    place_ref, normed_refs, cot_refs, bias_ref = refs[0], refs[1:3], refs[3:5], refs[5]
    piece_refs = refs[6 : 6 + pieces]
    grad_ref, full_ref, w_ref, qkv_ref, gm_ref, sems, out_sem = refs[6 + pieces :]
    tile = normed_refs[0].shape[0]
    part = w_ref.shape[1] // 4
    levels, pairs = bias_ref.shape[:2]
    scale = 1.0 / math.sqrt(head)
    copies = []
    for i, piece in enumerate(piece_refs):
        rows = pl.ds(pl.multiple_of(place_ref[i] * piece.shape[0], 16), piece.shape[0])
        copies.append(pltpu.make_async_copy(piece, w_ref.at[rows, :], sems.at[i]))
        copies[-1].start()
    for copy in copies:
        copy.wait()
    out_copy = pltpu.make_async_copy(w_ref, full_ref, out_sem)
    out_copy.start()
    for t in range(2):
        rows = pl.ds(t * tile, tile)
        for n in range(3):
            cols = pl.ds(n * part, part)
            qkv_ref[rows, cols] = jnp.dot(
                normed_refs[t][...], w_ref[:, cols], preferred_element_type=jnp.float32
            ).astype(jnp.bfloat16)
        gm_ref[rows, :] = jnp.dot(
            cot_refs[t][...], w_ref[:, 3 * part :], preferred_element_type=jnp.float32
        ).astype(jnp.bfloat16)
    lane = lax.broadcasted_iota(jnp.int32, (area, 2 * head), 1)
    left = lane < head

    def stacked(pair):
        zero = jnp.zeros_like(pair)
        return jnp.concatenate([jnp.where(left, pair, zero), jnp.where(left, zero, pair)], axis=0)

    def unstacked(product):
        return jnp.where(left, product[:area], product[area:]).astype(jnp.bfloat16)

    def across(a, b):
        return lax.dot_general(a, b, (((1,), (1,)), ((), ())), preferred_element_type=jnp.float32)

    def down(a, b):
        return lax.dot_general(a, b, (((0,), (0,)), ((), ())), preferred_element_type=jnp.float32)

    for w in range(2 * tile // area):
        rows = pl.ds(w * area, area)
        for p in range(pairs):
            at = p * 2 * head
            q_cols, k_cols, v_cols, m_cols = (pl.ds(n * part + at, 2 * head) for n in range(4))
            query = stacked(qkv_ref[rows, q_cols])
            keys = qkv_ref[rows, k_cols]
            values = qkv_ref[rows, v_cols]
            upstream = stacked(gm_ref[rows, q_cols])
            scores = across(query, keys) * scale + bias_ref[w % levels, p]
            expo = jnp.exp(scores - jnp.max(scores, axis=-1, keepdims=True))
            probs = expo / jnp.sum(expo, axis=-1, keepdims=True)
            probs_b = probs.astype(jnp.bfloat16)
            grad_ref[rows, m_cols] = unstacked(
                jnp.dot(probs_b, values, preferred_element_type=jnp.float32)
            )
            grad_probs = across(upstream, values)
            grad_ref[rows, v_cols] = down(probs_b, upstream).astype(jnp.bfloat16)
            inner = jnp.sum(probs * grad_probs, axis=-1, keepdims=True)
            grad_scores = (probs * (grad_probs - inner) * scale).astype(jnp.bfloat16)
            grad_ref[rows, q_cols] = unstacked(
                jnp.dot(grad_scores, keys, preferred_element_type=jnp.float32)
            )
            grad_ref[rows, k_cols] = down(grad_scores, query).astype(jnp.bfloat16)
    out_copy.wait()


def weights_kernel(turned_ref, own_ref, other_ref, *out_refs):
    rows, columns = out_refs[0].shape
    tokens = own_ref.shape[0]
    part = columns // 2
    for i in range(len(out_refs) // 2):
        for n in range(4):
            cols = pl.ds(n * part, part)
            kind = 1 if n == 3 else 0
            at = pl.ds(i * rows, rows)
            out_refs[2 * i + n // 2][:, pl.ds(n % 2 * part, part)] = (
                jnp.dot(turned_ref[kind, at, :tokens], own_ref[:, cols], preferred_element_type=jnp.float32)
                + jnp.dot(turned_ref[kind, at, tokens:], other_ref[:, cols], preferred_element_type=jnp.float32)
            ).astype(jnp.bfloat16)


def outer_kernel(grad_ref, w_ref, own_ref, other_ref):
    tile = own_ref.shape[0]
    width = w_ref.shape[0]
    part = w_ref.shape[1] // 4
    step = width // 4
    for n in range(4):
        rows = pl.ds(n * step, step)
        for k, w_cols in enumerate((pl.ds(3 * part, part), pl.ds(0, 3 * part))):
            product = lax.dot_general(
                grad_ref[:, w_cols], w_ref[rows, w_cols], (((1,), (1,)), ((), ())), preferred_element_type=jnp.float32
            )
            cols = pl.ds(k * width + n * step, step)
            own_ref[:, cols] = product[:tile]
            other_ref[:, cols] = product[tile:].astype(jnp.bfloat16)


def on_device(tokens, land, surface, gain, weights, shifts, index_table, bias_table, cotangent):
    levels, side, _, width = tokens.shape
    area = side * side
    tile = levels * area
    heads = bias_table.shape[2]
    entries = bias_table.shape[1]
    own_rows = weights.shape[0]
    part = weights.shape[1] // 8
    head = weights.shape[1] // 4 // heads
    own_heads = heads // 2
    far, near, beside, core = (lax.axis_index(axis) for axis in LON)
    grp = lax.axis_index("grp")
    first = near == 0
    f32 = jnp.float32

    def place(f, n, s, c):
        return ((far ^ f) * 4 + (near ^ n) * 2 + (beside ^ s)) * 2 + (core ^ c)

    halves = weights.reshape(own_rows, 4, 2, part)
    low = halves[:, :, 0].reshape(own_rows, 4 * part)
    high = halves[:, :, 1].reshape(own_rows, 4 * part)
    mine = jnp.where(first, low, high)
    came = swap(jnp.where(first, high, low), "near")
    flat_cot = cotangent.reshape(tile, width)
    surface_term = jnp.where(land[None, :, :, None] == 1, surface[1], surface[0])
    stream = (tokens.astype(f32) + surface_term).astype(jnp.bfloat16).reshape(tile, width)
    values = stream.astype(f32)
    center = values - jnp.mean(values, axis=-1, keepdims=True)
    spread = lax.rsqrt(jnp.mean(center * center, axis=-1, keepdims=True) + epsilon)
    normed = (center * spread * gain).astype(jnp.bfloat16)

    first_grp = grp == 0
    across_far = swap(jnp.where(first_grp, mine, came), "far")
    other_half = jnp.where(first_grp, 1, 0)
    far_side = swap(across_far, "side")
    found = [
        (mine, 0, 0, 0),
        (came, 0, 1, 0),
        (swap(mine, "side"), 0, 0, 1),
        (swap(came, "side"), 0, 1, 1),
        (across_far, 1, 1 - other_half, 0),
        (swap(across_far, "grp"), 1, other_half, 0),
        (far_side, 1, 1 - other_half, 1),
        (swap(far_side, "grp"), 1, other_half, 1),
    ]
    pieces = [piece for piece, *_ in found] + [swap(piece, "core") for piece, *_ in found]
    places = jnp.stack([place(f, n, s, c) for c in (0, 1) for _, f, n, s in found]).astype(jnp.int32)

    own_cot = roll_forward(flat_cot, shifts, levels, side)
    other_cot = swap(own_cot, "near")
    own_normed = roll_forward(normed, shifts, levels, side)
    other_normed = swap(own_normed, "near")

    def turned(own, other):
        both = jnp.concatenate([own, other], axis=0)
        full = jnp.concatenate([both, swap(both, "core")], axis=0).T
        blocks = full.reshape(-1, own_rows, full.shape[1])
        return jnp.concatenate(
            [
                lax.dynamic_index_in_dim(blocks, place(f, n, s, 0), 0, keepdims=False)
                for f in (1, 0)
                for s in (1, 0)
                for n in (1, 0)
            ],
            axis=0,
        )

    turned_both = jnp.stack([turned(own_normed, other_normed), turned(own_cot, other_cot)])

    onehot = (index_table[:, :, None] == jnp.arange(entries, dtype=jnp.int32)).astype(f32)
    own_table = lax.dynamic_slice_in_dim(bias_table, near * own_heads, own_heads, 2)
    bias = jnp.einsum("qkr,lrh->lhqk", onehot, own_table, precision=lax.Precision.HIGHEST)
    row_number = lax.axis_index("lat") * side + jnp.arange(side, dtype=jnp.int32)
    group = row_number[None, :] >= (side * lax.axis_size("lat") - shifts[:, 0])[:, None]
    group = jnp.repeat(group, side, axis=1)
    allowed = group[:, :, None] == group[:, None, :]
    bias = jnp.where(allowed[:, None], bias, -1e30).reshape(levels, own_heads // 2, 2 * area, area)

    vmem = pl.BlockSpec(memory_space=pltpu.VMEM)
    anywhere = pl.BlockSpec(memory_space=pl.ANY)
    grad, w_full = pl.pallas_call(
        functools.partial(attention_kernel, area, head, len(pieces)),
        out_shape=(
            jax.ShapeDtypeStruct((2 * tile, 4 * part), jnp.bfloat16),
            jax.ShapeDtypeStruct((width, 4 * part), jnp.bfloat16),
        ),
        in_specs=[pl.BlockSpec(memory_space=pltpu.SMEM)] + [vmem] * 5 + [anywhere] * len(pieces),
        out_specs=(vmem, anywhere),
        scratch_shapes=[
            pltpu.VMEM((width, 4 * part), jnp.bfloat16),
            pltpu.VMEM((2 * tile, 3 * part), jnp.bfloat16),
            pltpu.VMEM((2 * tile, part), jnp.bfloat16),
            pltpu.SemaphoreType.DMA((len(pieces),)),
            pltpu.SemaphoreType.DMA,
        ],
        compiler_params=pltpu.CompilerParams(vmem_limit_bytes=32 * 1024 * 1024),
        cost_estimate=pl.CostEstimate(flops=2_400_000_000, bytes_accessed=12_000_000, transcendentals=0),
        name="attention",
    )(places, own_normed, other_normed, own_cot, other_cot, bias, *pieces)

    blocks = pl.pallas_call(
        weights_kernel,
        out_shape=[jax.ShapeDtypeStruct((own_rows, 2 * part), jnp.bfloat16)] * 16,
        compiler_params=pltpu.CompilerParams(vmem_limit_bytes=32 * 1024 * 1024),
        cost_estimate=pl.CostEstimate(flops=2_400_000_000, bytes_accessed=6_000_000, transcendentals=0),
        name="weight_gradient",
    )(turned_both, grad, swap(grad, "core"))

    def block(f, s, n, h):
        return blocks[(((1 - f) * 2 + 1 - s) * 2 + 1 - n) * 2 + h]

    order = [(1, 0), (1, 1), (0, 0), (0, 1)]
    arrived = {}
    for n, h in order:
        added = block(1, 0, n, h).astype(f32) + swap(block(1, 1, n, h), "side").astype(f32)
        arrived[n, h] = swap(added.astype(jnp.bfloat16), "far")
    total = {}
    for n, h in order:
        total[n, h] = (
            block(0, 0, n, h).astype(f32)
            + swap(block(0, 1, n, h), "side").astype(f32)
            + arrived[n, h].astype(f32)
        )

    attended_own, attended_other = pl.pallas_call(
        outer_kernel,
        out_shape=(
            jax.ShapeDtypeStruct((tile, 2 * width), f32),
            jax.ShapeDtypeStruct((tile, 2 * width), jnp.bfloat16),
        ),
        compiler_params=pltpu.CompilerParams(vmem_limit_bytes=32 * 1024 * 1024),
        cost_estimate=pl.CostEstimate(flops=1_200_000_000, bytes_accessed=8_000_000, transcendentals=0),
        name="projections",
    )(grad, w_full)
    back = (attended_own + swap(attended_other, "near").astype(f32)).astype(jnp.bfloat16)
    back = roll_back(back, shifts, levels, side)
    output = (values + back[:, :width].astype(f32)).astype(jnp.bfloat16)
    scaled = center * spread
    upstream = back[:, width:].astype(f32) * gain
    grad_stream = spread * (
        upstream
        - jnp.mean(upstream, axis=-1, keepdims=True)
        - scaled * jnp.mean(upstream * scaled, axis=-1, keepdims=True)
    )
    grad_tokens = (flat_cot.astype(f32) + grad_stream).astype(jnp.bfloat16)

    theirs = [swap(total[1, h].astype(jnp.bfloat16), "near").astype(f32) for h in (0, 1)]
    token_count = tile * lax.axis_size("lat") * math.prod(lax.axis_size(axis) for axis in LON)
    columns = []
    for h in (0, 1):
        for k in (0, 1):
            kept = total[0, h][:, k * part : (k + 1) * part]
            other = theirs[h][:, k * part : (k + 1) * part]
            columns += [jnp.where(first, kept, other), jnp.where(first, other, kept)]
    summed = jnp.concatenate(columns, axis=1)
    if lax.axis_size("lat") > 1:
        summed = lax.psum(summed.astype(jnp.bfloat16), "lat").astype(f32)
    grad_weights = summed * (1.0 / math.sqrt(token_count))
    return (output.reshape(tokens.shape), grad_tokens.reshape(tokens.shape), grad_weights)


def solution(mesh):
    sizes = dict(mesh.shape)
    devices = mesh.devices.reshape(sizes["grp"], sizes["lon"] // 8, 2, 2, 2, sizes["lat"])
    finer = Mesh(devices, ("grp",) + LON + ("lat",))
    return jax.shard_map(
        on_device,
        mesh=finer,
        in_specs=(
            P("grp", "lat", LON, None),
            P(("grp", "lat"), LON),
            P(),
            P(),
            P(LON, None),
            P(),
            P(),
            P("lat", None, None),
            P("grp", "lat", LON, None),
        ),
        out_specs=(
            P("grp", "lat", LON, None),
            P("grp", "lat", LON, None),
            P(("grp",) + LON, None),
        ),
        check_vma=False,
    )
```

time: 232 us -> 189 us (0.81)
  waiting for transfers between devices: 158 us -> 73.1 us
  starting transfers between devices: 8.37 us -> 38.3 us
  between operations: 14.5 us -> 1.22 us
  Pallas kernels: 12.2 us -> 19.7 us
  other arithmetic: 7.1 us -> 14 us
  matrix products: 9.38 us -> 14.8 us
  local copies, waits for them, and re-layouts: 19.6 us -> 24.6 us
    reduce_scatter x1 -> x0, waiting for transfers between devices: 77.2 us -> none  [on_device(): lax.psum_scatter(grad_tile, 'chip', scatter_dimension=0, tiled=True)]
    ppermute x4 -> x35, waiting for transfers between devices: 3.98 us -> 73.1 us  [swap(): return lax.ppermute(shard, axis, [(0, 1), (1, 0)])]
    all_gather x1 -> x0, waiting for transfers between devices: 53.5 us -> none  [on_device(): w_own = lax.all_gather(chip_rows, 'chip', axis=0, tiled=True)]
    ppermute x4 -> x35, starting transfers between devices: 7.62 us -> 36.3 us  [swap(): return lax.ppermute(shard, axis, [(0, 1), (1, 0)])]
    ppermute x2 -> x3, waiting for transfers between devices: 23.8 us -> 0.01 us  [along_lon(): lax.ppermute(shard, LON, [(i, (i + by) % count) for i in range(count)])]
    pallas_call x1 -> x2, Pallas kernels: 10.2 us -> 15.6 us  [the longest x1 12.2 us: on_device(): pl.pallas_call(functools.partial(attention_kernel, area, head, len(pieces...]
    transpose x0 -> x2, local copies, waits for them, and re-layouts: none -> 5.32 us  [turned(): full = jnp.concatenate([both, swap(both, 'core')], axis=0).T]
    transpose x0 -> x2, other arithmetic: none -> 4.76 us  [turned(): full = jnp.concatenate([both, swap(both, 'core')], axis=0).T]
  transfers between devices with their start and end apart: 8 -> 38, of which waited for: 7 -> 14; matrix products, arithmetic and copies ran while one was open for 7% -> 21% of each run, Pallas kernels for 1% -> 11%
where the time goes in v2:
time: 189 us; the launch traced here: 186 us
  waiting for transfers between devices  73.1 us (39%)
  starting transfers between devices  38.3 us (20%)
  local copies, waits for them, and re-layouts  24.6 us (13%)
  Pallas kernels  19.7 us (10%)
  matrix products  14.8 us (8%)
  other arithmetic  14 us (7%)
    ppermute x35, waiting for transfers between devices, swap(): return lax.ppermute(shard, axis, [(0, 1), (1, 0)])  73.1 us
    ppermute x35, starting transfers between devices, swap(): return lax.ppermute(shard, axis, [(0, 1), (1, 0)])  36.3 us
    unnamed x52, local copies, waits for them, and re-layouts  12.5 us
    pallas_call x1, Pallas kernels, on_device(): pl.pallas_call(functools.partial(attention_kernel, area, head, len(pieces...  12.2 us
    dot_general x3, matrix products, picked(): jnp.dot(onehot, both, preferred_element_type=jnp.float32)  11.2 us
    transpose x2, local copies, waits for them, and re-layouts, turned(): full = jnp.concatenate([both, swap(both, 'core')], axis=0).T  5.32 us
    transpose x2, other arithmetic, turned(): full = jnp.concatenate([both, swap(both, 'core')], axis=0).T  4.76 us
    pallas_call x1, Pallas kernels, on_device(): pl.pallas_call(outer_kernel, out_shape=(jax.ShapeDtypeStruct((tile, 2 * w...  4.07 us
  transfers between devices with their start and end apart: 38, of which 14 were waited for; matrix products, arithmetic and copies ran while one was open for 21% of the time, Pallas kernels for 11%

profile of v2, /device:TPU:6, one launch (start us, length us, event | category | flops | bytes accessed | tf_op | source)
XLA Modules:
  0.0 185.7 jit_solution(9814052889711036141)
XLA Ops:
  0.7 2.2 %reshape.108 = bf16[96,4,2,384]{3,2,1,0:T(2,128)(2,1)S(1)} reshape(bf16[96,3072]{1,0:T(8,128)(2,1)} %param.13) | data formatting | bytes 1179648 | tf_op jit(solution)/shard_map/reshape | solution.py:197
  10.3 6.5 %collective-permute-done.4.refs_7_ = bf16[96,1536]{1,0:T(8,128)(2,1)S(1)} collective-permute-done((bf16[96,1536]{1,0:T(8,128)(2,1)S(1)}, bf16[96,1536]{1,0:T(8,128)(2,1)S(1)}, u32[]{:S(2)}, u32[]{:S(2)}) %collective-permute-start.4) | collective-permute-done | bytes 294944 | tf_op jit(solution)/shard_map/ppermute | solution.py:27
  16.8 2.7 %collective-permute-start.7 = (bf16[96,1536]{1,0:T(8,128)(2,1)S(1)}, bf16[96,1536]{1,0:T(8,128)(2,1)S(1)}, u32[]{:S(2)}, u32[]{:S(2)}) collective-permute-start(bf16[96,1536]{1,0:T(8,128)(2,1)S(1)} %broadcast_select_fusion), channel_id=1, source_target_pairs={{0,8},{8,0},{1,9},{9,1},{2,10},{10,2},{3,11},{11,3},{4,12},{12,4},... | collective-permute-start | bytes 884744 | tf_op jit(solution)/shard_map/ppermute | solution.py:27
  19.4 2.6 %collective-permute-done.5.refs_8_ = bf16[96,1536]{1,0:T(8,128)(2,1)S(1)} collective-permute-done((bf16[96,1536]{1,0:T(8,128)(2,1)S(1)}, bf16[96,1536]{1,0:T(8,128)(2,1)S(1)}, u32[]{:S(2)}, u32[]{:S(2)}) %collective-permute-start.5) | collective-permute-done | bytes 294944 | tf_op jit(solution)/shard_map/ppermute | solution.py:27
  22.6 3.9 %convolution_convert_fusion.2.refs_1_ = bf16[128,1536]{1,0:T(8,128)(2,1)S(1)} fusion(bf16[128,1536]{1,0:T(8,128)(2,1)} %collective-permute-done, bf16[128,1536]{1,0:T(8,128)(2,1)S(1)} %fusion.22, s32[]{:T(128)} %bitcast.24, s32[]{:T(128)} %bitcast.23, s32[]{:T(128)} %bitcast.22, s32[]{:T(128)} %bitcast.21, s32[128]{0:T(128)S(1)} %get-tuple-element.69, ...), kind=kOutput, calls=%fused_computation.5 | convolution fusion | flops 104267776 | bytes 1183120 | tf_op jit(solution)/shard_map/dot_general | solution.py:52
  28.2 4.1 %convolution_convert_fusion.1.refs_3_ = bf16[128,1536]{1,0:T(8,128)(2,1)S(1)} fusion(bf16[128,1536]{1,0:T(8,128)(2,1)} %collective-permute-done.2, bf16[128,1536]{1,0:T(8,128)(2,1)} %bitcast.25, s32[]{:T(128)} %bitcast.24, s32[]{:T(128)} %bitcast.23, s32[]{:T(128)} %bitcast.22, s32[]{:T(128)} %bitcast.21, s32[128]{0:T(128)S(1)} %get-tuple-element.69, ...), kind=kOutput, calls=%fused_computation.4 | convolution fusion | flops 104267776 | bytes 1183120 | tf_op jit(solution)/shard_map/dot_general | solution.py:52
  32.2 6.3 %collective-permute-start.6 = (bf16[96,1536]{1,0:T(8,128)(2,1)S(1)}, bf16[96,1536]{1,0:T(8,128)(2,1)}, u32[]{:S(2)}, u32[]{:S(2)}) collective-permute-start(bf16[96,1536]{1,0:T(8,128)(2,1)S(1)} %collective-permute-done.4.refs_7_), channel_id=1, source_target_pairs={{0,2},{2,0},{1,3},{3,1},{4,6},{6,4},{5,7},{7,5},{8,10},{10,8},{9,1... | collective-permute-start | bytes 884744 | tf_op jit(solution)/shard_map/ppermute | solution.py:27
  40.4 6.1 %collective-permute-done.6.refs_9_ = bf16[96,1536]{1,0:T(8,128)(2,1)} collective-permute-done((bf16[96,1536]{1,0:T(8,128)(2,1)S(1)}, bf16[96,1536]{1,0:T(8,128)(2,1)}, u32[]{:S(2)}, u32[]{:S(2)}) %collective-permute-start.6) | collective-permute-done | bytes 294944 | tf_op jit(solution)/shard_map/ppermute | solution.py:27
  47.0 4.9 %collective-permute-done.9.refs_12_ = bf16[96,1536]{1,0:T(8,128)(2,1)} collective-permute-done((bf16[96,1536]{1,0:T(8,128)(2,1)S(1)}, bf16[96,1536]{1,0:T(8,128)(2,1)}, u32[]{:S(2)}, u32[]{:S(2)}) %collective-permute-start.9) | collective-permute-done | bytes 294944 | tf_op jit(solution)/shard_map/ppermute | solution.py:27
  56.8 3.5 %collective-permute-done.10.refs_13_ = bf16[96,1536]{1,0:T(8,128)(2,1)} collective-permute-done((bf16[96,1536]{1,0:T(8,128)(2,1)}, bf16[96,1536]{1,0:T(8,128)(2,1)}, u32[]{:S(2)}, u32[]{:S(2)}) %collective-permute-start.10) | collective-permute-done | bytes 294944 | tf_op jit(solution)/shard_map/ppermute | solution.py:27
  60.4 3.6 %fusion.7 = f32[2,6,64,64]{3,1,2,0:T(8,128)} fusion(s32[64,64]{1,0:T(8,128)S(1)} %copy-done.17, pred[2,64,64]{2,1,0:T(8,128)(4,1)S(1)} %broadcast_compare_fusion, f32[2,225,6]{1,0,2:T(2,128)S(1)} %constant_dynamic-slice_fusion), kind=kOutput, calls=%fused_computation.14 | convolution fusion | flops 133681152 | bytes 231984 | tf_op jit(solution)/shard_map/qkr,lrh->lhqk/dot_general | solution.py:250
  69.7 12.2 %attention.1 = (bf16[256,1536]{1,0:T(8,128)(2,1)}, bf16[1536,1536]{1,0:T(8,128)(2,1)S(1)}) custom-call(s32[16]{0:T(128)S(1)} %stack.76.refs_0_, bf16[128,1536]{1,0:T(8,128)(2,1)S(1)} %convolution_convert_fusion.2.refs_1_, bf16[128,1536]{1,0:T(8,128)(2,1)S(1)} %collective-permute-done.1.refs_2_, bf16[128,1536]{1,0:T(8,128)(2,1)S(1)} %convolution_convert_fusion.1.refs_3_, ...), custom_call_target="tpu_custom_call" | custom-call | flops 2400000000 | bytes 12000000 | tf_op jit(solution)/shard_map/attention/pallas_call | solution.py:259
  82.4 4.1 %projections.1 = (f32[128,3072]{1,0:T(8,128)S(1)}, bf16[128,3072]{1,0:T(8,128)(2,1)}) custom-call(bf16[256,1536]{1,0:T(8,128)(2,1)} %get-tuple-element.23.grad_ref.own_ref, bf16[1536,1536]{1,0:T(8,128)(2,1)S(1)} %get-tuple-element.24.w_ref), custom_call_target="tpu_custom_call" | custom-call | flops 1200000000 | bytes 8000000 | tf_op jit(solution)/shard_map/projections/pallas_call | solution.py:303
  86.9 2.4 %maximum_bitcast_fusion = bf16[1536,512]{0,1:T(8,128)(2,1)} fusion(bf16[256,1536]{1,0:T(8,128)(2,1)} %collective-permute-done.21, bf16[128,1536]{1,0:T(8,128)(2,1)S(1)} %collective-permute-done.1.refs_2_, bf16[128,1536]{1,0:T(8,128)(2,1)S(1)} %convolution_convert_fusion.2.refs_1_), kind=kLoop, calls=%fused_computation.10 | loop fusion | flops 4718592 | bytes 3145728 | tf_op jit(solution)/shard_map/transpose | solution.py:234
  89.2 2.6 %copy.36 = bf16[1536,512]{1,0:T(8,128)(2,1)} copy(bf16[1536,512]{0,1:T(8,128)(2,1)} %maximum_bitcast_fusion) | data formatting | bytes 3145728 | tf_op jit(solution)/shard_map/transpose | solution.py:234
  91.9 2.4 %maximum_bitcast_fusion.1 = bf16[1536,512]{0,1:T(8,128)(2,1)} fusion(bf16[256,1536]{1,0:T(8,128)(2,1)} %collective-permute-done.22, bf16[128,1536]{1,0:T(8,128)(2,1)S(1)} %collective-permute-done.3.refs_4_, bf16[128,1536]{1,0:T(8,128)(2,1)S(1)} %convolution_convert_fusion.1.refs_3_), kind=kLoop, calls=%fused_computation.11 | loop fusion | flops 4718592 | bytes 3145728 | tf_op jit(solution)/shard_map/transpose | solution.py:234
  94.2 2.7 %copy.37 = bf16[1536,512]{1,0:T(8,128)(2,1)} copy(bf16[1536,512]{0,1:T(8,128)(2,1)} %maximum_bitcast_fusion.1) | data formatting | bytes 3145728 | tf_op jit(solution)/shard_map/transpose | solution.py:234
  104.5 3.5 %weight_gradient.1 = (bf16[96,768]{1,0:T(8,128)(2,1)S(1)}, bf16[96,768]{1,0:T(8,128)(2,1)S(1)}, bf16[96,768]{1,0:T(8,128)(2,1)S(1)}, bf16[96,768]{1,0:T(8,128)(2...) custom-call(bf16[2,768,512]{2,1,0:T(8,128)(2,1)S(1)} %pad_maximum_fu, ...), custom_call_target="tpu_custom_call" | custom-call | flops 2400000000 | bytes 6000000 | tf_op jit(solution)/shard_map/weight_gradient/pallas_call | solution.py:279
  115.2 15.1 %collective-permute-done.28 = bf16[96,768]{1,0:T(8,128)(2,1)S(1)} collective-permute-done((bf16[96,768]{1,0:T(8,128)(2,1)S(1)}, bf16[96,768]{1,0:T(8,128)(2,1)S(1)}, u32[]{:S(2)}, u32[]{:S(2)}) %collective-permute-start.28) | collective-permute-done | bytes 147488 | tf_op jit(solution)/shard_map/ppermute | solution.py:27
  130.3 2.5 %collective-permute-start.32 = (bf16[96,768]{1,0:T(8,128)(2,1)S(1)}, bf16[96,768]{1,0:T(8,128)(2,1)S(1)}, u32[]{:S(2)}, u32[]{:S(2)}) collective-permute-start(bf16[96,768]{1,0:T(8,128)(2,1)S(1)} %get-tuple-element.38), channel_id=1, source_target_pairs={{0,2},{2,0},{1,3},{3,1},{4,6},{6,4},{5,7},{7,5},{8,10},{10,8},{9,1... | collective-permute-start | bytes 442376 | tf_op jit(solution)/shard_map/ppermute | solution.py:27
  132.8 4.5 %collective-permute-done.32 = bf16[96,768]{1,0:T(8,128)(2,1)S(1)} collective-permute-done((bf16[96,768]{1,0:T(8,128)(2,1)S(1)}, bf16[96,768]{1,0:T(8,128)(2,1)S(1)}, u32[]{:S(2)}, u32[]{:S(2)}) %collective-permute-start.32) | collective-permute-done | bytes 147488 | tf_op jit(solution)/shard_map/ppermute | solution.py:27
  137.3 2.2 %collective-permute-start.35 = (bf16[96,768]{1,0:T(8,128)(2,1)S(1)}, bf16[96,768]{1,0:T(8,128)(2,1)S(1)}, u32[]{:S(2)}, u32[]{:S(2)}) collective-permute-start(bf16[96,768]{1,0:T(8,128)(2,1)S(1)} %get-tuple-element.42), channel_id=1, source_target_pairs={{0,2},{2,0},{1,3},{3,1},{4,6},{6,4},{5,7},{7,5},{8,10},{10,8},{9,1... | collective-permute-start | bytes 442376 | tf_op jit(solution)/shard_map/ppermute | solution.py:27
  139.5 4.3 %collective-permute-done.35 = bf16[96,768]{1,0:T(8,128)(2,1)S(1)} collective-permute-done((bf16[96,768]{1,0:T(8,128)(2,1)S(1)}, bf16[96,768]{1,0:T(8,128)(2,1)S(1)}, u32[]{:S(2)}, u32[]{:S(2)}) %collective-permute-start.35) | collective-permute-done | bytes 147488 | tf_op jit(solution)/shard_map/ppermute | solution.py:27
  143.8 2.5 %collective-permute-start.29 = (bf16[96,768]{1,0:T(8,128)(2,1)S(1)}, bf16[96,768]{1,0:T(8,128)(2,1)S(1)}, u32[]{:S(2)}, u32[]{:S(2)}) collective-permute-start(bf16[96,768]{1,0:T(8,128)(2,1)S(1)} %add_convert_fusion.6), channel_id=1, source_target_pairs={{0,8},{8,0},{1,9},{9,1},{2,10},{10,2},{3,11},{11,3},{4,12},{12,4},... | collective-permute-start | bytes 442376 | tf_op jit(solution)/shard_map/ppermute | solution.py:27
  147.8 5.6 %collective-permute-done.29 = bf16[96,768]{1,0:T(8,128)(2,1)S(1)} collective-permute-done((bf16[96,768]{1,0:T(8,128)(2,1)S(1)}, bf16[96,768]{1,0:T(8,128)(2,1)S(1)}, u32[]{:S(2)}, u32[]{:S(2)}) %collective-permute-start.29) | collective-permute-done | bytes 147488 | tf_op jit(solution)/shard_map/ppermute | solution.py:27
  153.5 3.0 %collective-permute-start.26 = (bf16[96,768]{1,0:T(8,128)(2,1)S(1)}, bf16[96,768]{1,0:T(8,128)(2,1)S(1)}, u32[]{:S(2)}, u32[]{:S(2)}) collective-permute-start(bf16[96,768]{1,0:T(8,128)(2,1)S(1)} %add_convert_fusion.7), channel_id=1, source_target_pairs={{0,8},{8,0},{1,9},{9,1},{2,10},{10,2},{3,11},{11,3},{4,12},{12,4},... | collective-permute-start | bytes 442376 | tf_op jit(solution)/shard_map/ppermute | solution.py:27
  156.5 10.7 %collective-permute-done.36 = bf16[96,768]{1,0:T(8,128)(2,1)S(1)} collective-permute-done((bf16[96,768]{1,0:T(8,128)(2,1)S(1)}, bf16[96,768]{1,0:T(8,128)(2,1)S(1)}, u32[]{:S(2)}, u32[]{:S(2)}) %collective-permute-start.36) | collective-permute-done | bytes 147488 | tf_op jit(solution)/shard_map/ppermute | solution.py:27
  167.3 1.8 collective-permute-start.30
  169.1 4.3 %collective-permute-done.26 = bf16[96,768]{1,0:T(8,128)(2,1)S(1)} collective-permute-done((bf16[96,768]{1,0:T(8,128)(2,1)S(1)}, bf16[96,768]{1,0:T(8,128)(2,1)S(1)}, u32[]{:S(2)}, u32[]{:S(2)}) %collective-permute-start.26) | collective-permute-done | bytes 147488 | tf_op jit(solution)/shard_map/ppermute | solution.py:27
  176.7 1.8 collective-permute-done.37
  179.7 3.2 %convolution_convert_fusion = bf16[128,3072]{1,0:T(8,128)(2,1)S(1)} fusion(bf16[128,3072]{1,0:T(8,128)(2,1)S(1)} %add_convert_fusion, bf16[128,3072]{1,0:T(8,128)(2,1)S(1)} %collective-permute-done.20, s32[]{:T(128)} %bitcast.4, s32[]{:T(128)} %bitcast.3, s32[128]{0:T(128)S(1)} %get-tuple-element.69, s32[128]{0:T(128)S(1)} %get-tuple-element.71, ...), kind=kOutput, calls=%fused_computation.3 | convolution fusion | flops 206700544 | bytes 2362768 | tf_op jit(solution)/shard_map/dot_general | solution.py:52
  183.3 2.3 %fusion.27 = (bf16[128,1536]{1,0:T(8,128)(2,1)}, bf16[128,1536]{1,0:T(8,128)(2,1)}) fusion(bf16[2,8,8,1536]{3,2,1,0:T(8,128)(2,1)S(1)} %copy-done.10, f32[128]{0:T(128)S(1)} %broadcast_multiply_fusion.2, f32[128]{0:T(128)S(1)} %broadcast_multiply_fusion.3, f32[1536]{0:T(1024)S(1)} %copy-done.13, f32[128]{0:T(128)S(1)} %rsqrt.12, f32[128]{0:T(128)S(1)} %div.82, ...), kind=kLoop, calls=%fused_computation.38 | loop fusion | flops 2949120 | bytes 2367488 | tf_op jit(solution)/shard_map/convert_element_type | solution.py:323
  (165 shorter events, 44.5 us)
Async XLA Ops:
  4.1 28.1 %collective-permute-start.11 = (bf16[96,1536]{1,0:T(8,128)(2,1)S(1)}, bf16[96,1536]{1,0:T(8,128)(2,1)S(1)}, u32[]{:S(2)}, u32[]{:S(2)}) collective-permute-start(bf16[96,1536]{1,0:T(8,128)(2,1)S(1)} %bitcast.112), channel_id=1, source_target_pairs={{0,1},{1,0},{2,3},{3,2},{4,5},{5,4},{6,7},{7,6},{8,9},{9,8},{10,11... | collective-permute-start | bytes 884744 | tf_op jit(solution)/shard_map/ppermute | solution.py:27
  4.2 17.9 %collective-permute-start.5 = (bf16[96,1536]{1,0:T(8,128)(2,1)S(1)}, bf16[96,1536]{1,0:T(8,128)(2,1)S(1)}, u32[]{:S(2)}, u32[]{:S(2)}) collective-permute-start(bf16[96,1536]{1,0:T(8,128)(2,1)S(1)} %bitcast.113), channel_id=1, source_target_pairs={{0,2},{2,0},{1,3},{3,1},{4,6},{6,4},{5,7},{7,5},{8,10},{10,8},{9,1... | collective-permute-start | bytes 884744 | tf_op jit(solution)/shard_map/ppermute | solution.py:27
  5.9 16.2 %collective-permute-start = (bf16[128,1536]{1,0:T(8,128)(2,1)S(1)}, bf16[128,1536]{1,0:T(8,128)(2,1)}, u32[]{:S(2)}, u32[]{:S(2)}) collective-permute-start(bf16[128,1536]{1,0:T(8,128)(2,1)S(1)} %fusion.22), channel_id=1, source_target_pairs={{0,15},{1,0},{2,1},{3,2},{4,3},{5,4},{6,5},{7,6},{8,7},{9,8},{10,9... | collective-permute-start | bytes 1179656 | tf_op jit(solution)/shard_map/ppermute | solution.py:18
  7.2 19.3 %collective-permute-start.2 = (bf16[128,1536]{1,0:T(8,128)(2,1)}, bf16[128,1536]{1,0:T(8,128)(2,1)}, u32[]{:S(2)}, u32[]{:S(2)}) collective-permute-start(bf16[128,1536]{1,0:T(8,128)(2,1)} %bitcast.25), channel_id=1, source_target_pairs={{0,15},{1,0},{2,1},{3,2},{4,3},{5,4},{6,5},{7,6},{8,7},{9,8},{10,9... | collective-permute-start | bytes 1179656 | tf_op jit(solution)/shard_map/ppermute | solution.py:18
  7.6 9.1 %collective-permute-start.4 = (bf16[96,1536]{1,0:T(8,128)(2,1)S(1)}, bf16[96,1536]{1,0:T(8,128)(2,1)S(1)}, u32[]{:S(2)}, u32[]{:S(2)}) collective-permute-start(bf16[96,1536]{1,0:T(8,128)(2,1)S(1)} %bitcast.139), channel_id=1, source_target_pairs={{0,4},{4,0},{1,5},{5,1},{2,6},{6,2},{3,7},{7,3},{8,12},{12,8},{9,1... | collective-permute-start | bytes 884744 | tf_op jit(solution)/shard_map/ppermute | solution.py:27
  16.8 22.8 %collective-permute-start.7 = (bf16[96,1536]{1,0:T(8,128)(2,1)S(1)}, bf16[96,1536]{1,0:T(8,128)(2,1)S(1)}, u32[]{:S(2)}, u32[]{:S(2)}) collective-permute-start(bf16[96,1536]{1,0:T(8,128)(2,1)S(1)} %broadcast_select_fusion), channel_id=1, source_target_pairs={{0,8},{8,0},{1,9},{9,1},{2,10},{10,2},{3,11},{11,3},{4,12},{12,4},... | collective-permute-start | bytes 884744 | tf_op jit(solution)/shard_map/ppermute | solution.py:27
  22.0 18.2 %collective-permute-start.12 = (bf16[96,1536]{1,0:T(8,128)(2,1)S(1)}, bf16[96,1536]{1,0:T(8,128)(2,1)}, u32[]{:S(2)}, u32[]{:S(2)}) collective-permute-start(bf16[96,1536]{1,0:T(8,128)(2,1)S(1)} %collective-permute-done.4.refs_7_), channel_id=1, source_target_pairs={{0,1},{1,0},{2,3},{3,2},{4,5},{5,4},{6,7},{7,6},{8,9},{9,8},{10,11... | collective-permute-start | bytes 884744 | tf_op jit(solution)/shard_map/ppermute | solution.py:27
  22.0 16.5 %collective-permute-start.13 = (bf16[96,1536]{1,0:T(8,128)(2,1)S(1)}, bf16[96,1536]{1,0:T(8,128)(2,1)S(1)}, u32[]{:S(2)}, u32[]{:S(2)}) collective-permute-start(bf16[96,1536]{1,0:T(8,128)(2,1)S(1)} %collective-permute-done.5.refs_8_), channel_id=1, source_target_pairs={{0,1},{1,0},{2,3},{3,2},{4,5},{5,4},{6,7},{7,6},{8,9},{9,8},{10,11... | collective-permute-start | bytes 884744 | tf_op jit(solution)/shard_map/ppermute | solution.py:27
  26.5 20.5 %collective-permute-start.1 = (bf16[128,1536]{1,0:T(8,128)(2,1)S(1)}, bf16[128,1536]{1,0:T(8,128)(2,1)S(1)}, u32[]{:S(2)}, u32[]{:S(2)}) collective-permute-start(bf16[128,1536]{1,0:T(8,128)(2,1)S(1)} %convolution_convert_fusion.2.refs_1_), channel_id=1, source_target_pairs={{0,4},{4,0},{1,5},{5,1},{2,6},{6,2},{3,7},{7,3},{8,12},{12,8},{9,1... | collective-permute-start | bytes 1179656 | tf_op jit(solution)/shard_map/ppermute | solution.py:27
  32.2 14.2 %collective-permute-start.6 = (bf16[96,1536]{1,0:T(8,128)(2,1)S(1)}, bf16[96,1536]{1,0:T(8,128)(2,1)}, u32[]{:S(2)}, u32[]{:S(2)}) collective-permute-start(bf16[96,1536]{1,0:T(8,128)(2,1)S(1)} %collective-permute-done.4.refs_7_), channel_id=1, source_target_pairs={{0,2},{2,0},{1,3},{3,1},{4,6},{6,4},{5,7},{7,5},{8,10},{10,8},{9,1... | collective-permute-start | bytes 884744 | tf_op jit(solution)/shard_map/ppermute | solution.py:27
  39.3 14.2 %collective-permute-start.3 = (bf16[128,1536]{1,0:T(8,128)(2,1)S(1)}, bf16[128,1536]{1,0:T(8,128)(2,1)S(1)}, u32[]{:S(2)}, u32[]{:S(2)}) collective-permute-start(bf16[128,1536]{1,0:T(8,128)(2,1)S(1)} %convolution_convert_fusion.1.refs_3_), channel_id=1, source_target_pairs={{0,4},{4,0},{1,5},{5,1},{2,6},{6,2},{3,7},{7,3},{8,12},{12,8},{9,1... | collective-permute-start | bytes 1179656 | tf_op jit(solution)/shard_map/ppermute | solution.py:27
  39.6 12.3 %collective-permute-start.9 = (bf16[96,1536]{1,0:T(8,128)(2,1)S(1)}, bf16[96,1536]{1,0:T(8,128)(2,1)}, u32[]{:S(2)}, u32[]{:S(2)}) collective-permute-start(bf16[96,1536]{1,0:T(8,128)(2,1)S(1)} %collective-permute-done.7.refs_10_), channel_id=1, source_target_pairs={{0,2},{2,0},{1,3},{3,1},{4,6},{6,4},{5,7},{7,5},{8,10},{10,8},{9,1... | collective-permute-start | bytes 884744 | tf_op jit(solution)/shard_map/ppermute | solution.py:27
  40.3 14.1 %collective-permute-start.15 = (bf16[96,1536]{1,0:T(8,128)(2,1)S(1)}, bf16[96,1536]{1,0:T(8,128)(2,1)S(1)}, u32[]{:S(2)}, u32[]{:S(2)}) collective-permute-start(bf16[96,1536]{1,0:T(8,128)(2,1)S(1)} %collective-permute-done.7.refs_10_), channel_id=1, source_target_pairs={{0,1},{1,0},{2,3},{3,2},{4,5},{5,4},{6,7},{7,6},{8,9},{9,8},{10,11... | collective-permute-start | bytes 884744 | tf_op jit(solution)/shard_map/ppermute | solution.py:27
  46.5 9.1 %collective-permute-start.8 = (bf16[96,1536]{1,0:T(8,128)(2,1)S(1)}, bf16[96,1536]{1,0:T(8,128)(2,1)}, u32[]{:S(2)}, u32[]{:S(2)}) collective-permute-start(bf16[96,1536]{1,0:T(8,128)(2,1)S(1)} %collective-permute-done.7.refs_10_), channel_id=1, source_target_pairs={{0,16},{16,0},{1,17},{17,1},{2,18},{18,2},{3,19},{19,3},{4,20},{20... | collective-permute-start | bytes 884744 | tf_op jit(solution)/shard_map/ppermute | solution.py:27
  47.0 8.6 %collective-permute-start.14 = (bf16[96,1536]{1,0:T(8,128)(2,1)}, bf16[96,1536]{1,0:T(8,128)(2,1)S(1)}, u32[]{:S(2)}, u32[]{:S(2)}) collective-permute-start(bf16[96,1536]{1,0:T(8,128)(2,1)} %collective-permute-done.6.refs_9_), channel_id=1, source_target_pairs={{0,1},{1,0},{2,3},{3,2},{4,5},{5,4},{6,7},{7,6},{8,9},{9,8},{10,11... | collective-permute-start | bytes 884744 | tf_op jit(solution)/shard_map/ppermute | solution.py:27
  51.9 8.5 %collective-permute-start.10 = (bf16[96,1536]{1,0:T(8,128)(2,1)}, bf16[96,1536]{1,0:T(8,128)(2,1)}, u32[]{:S(2)}, u32[]{:S(2)}) collective-permute-start(bf16[96,1536]{1,0:T(8,128)(2,1)} %collective-permute-done.9.refs_12_), channel_id=1, source_target_pairs={{0,16},{16,0},{1,17},{17,1},{2,18},{18,2},{3,19},{19,3},{4,20},{20... | collective-permute-start | bytes 884744 | tf_op jit(solution)/shard_map/ppermute | solution.py:27
  53.4 33.4 %collective-permute-start.21 = (bf16[256,1536]{1,0:T(8,128)(2,1)}, bf16[256,1536]{1,0:T(8,128)(2,1)}, u32[]{:S(2)}, u32[]{:S(2)}) collective-permute-start(bf16[256,1536]{1,0:T(8,128)(2,1)} %pad_maximum_fusion.1), channel_id=1, source_target_pairs={{0,1},{1,0},{2,3},{3,2},{4,5},{5,4},{6,7},{7,6},{8,9},{9,8},{10,11... | collective-permute-start | bytes 2359304 | tf_op jit(solution)/shard_map/ppermute | solution.py:27
  55.1 36.8 %collective-permute-start.22 = (bf16[256,1536]{1,0:T(8,128)(2,1)}, bf16[256,1536]{1,0:T(8,128)(2,1)}, u32[]{:S(2)}, u32[]{:S(2)}) collective-permute-start(bf16[256,1536]{1,0:T(8,128)(2,1)} %pad_maximum_fusion.2), channel_id=1, source_target_pairs={{0,1},{1,0},{2,3},{3,2},{4,5},{5,4},{6,7},{7,6},{8,9},{9,8},{10,11... | collective-permute-start | bytes 2359304 | tf_op jit(solution)/shard_map/ppermute | solution.py:27
  55.6 10.2 %collective-permute-start.17 = (bf16[96,1536]{1,0:T(8,128)(2,1)}, bf16[96,1536]{1,0:T(8,128)(2,1)}, u32[]{:S(2)}, u32[]{:S(2)}) collective-permute-start(bf16[96,1536]{1,0:T(8,128)(2,1)} %collective-permute-done.9.refs_12_), channel_id=1, source_target_pairs={{0,1},{1,0},{2,3},{3,2},{4,5},{5,4},{6,7},{7,6},{8,9},{9,8},{10,11... | collective-permute-start | bytes 884744 | tf_op jit(solution)/shard_map/ppermute | solution.py:27
  56.3 9.5 %collective-permute-start.16 = (bf16[96,1536]{1,0:T(8,128)(2,1)}, bf16[96,1536]{1,0:T(8,128)(2,1)}, u32[]{:S(2)}, u32[]{:S(2)}) collective-permute-start(bf16[96,1536]{1,0:T(8,128)(2,1)} %collective-permute-done.8.refs_11_), channel_id=1, source_target_pairs={{0,1},{1,0},{2,3},{3,2},{4,5},{5,4},{6,7},{7,6},{8,9},{9,8},{10,11... | collective-permute-start | bytes 884744 | tf_op jit(solution)/shard_map/ppermute | solution.py:27
  81.9 22.6 %collective-permute-start.23 = (bf16[256,1536]{1,0:T(8,128)(2,1)}, bf16[256,1536]{1,0:T(8,128)(2,1)}, u32[]{:S(2)}, u32[]{:S(2)}) collective-permute-start(bf16[256,1536]{1,0:T(8,128)(2,1)} %get-tuple-element.23.grad_ref.own_ref), channel_id=1, source_target_pairs={{0,1},{1,0},{2,3},{3,2},{4,5},{5,4},{6,7},{7,6},{8,9},{9,8},{10,11... | collective-permute-start | bytes 2359304 | tf_op jit(solution)/shard_map/ppermute | solution.py:27
  86.5 22.9 %collective-permute-start.19 = (bf16[128,3072]{1,0:T(8,128)(2,1)}, bf16[128,3072]{1,0:T(8,128)(2,1)}, u32[]{:S(2)}, u32[]{:S(2)}) collective-permute-start(bf16[128,3072]{1,0:T(8,128)(2,1)} %get-tuple-element.26), channel_id=1, source_target_pairs={{0,4},{4,0},{1,5},{5,1},{2,6},{6,2},{3,7},{7,3},{8,12},{12,8},{9,1... | collective-permute-start | bytes 2359304 | tf_op jit(solution)/shard_map/ppermute | solution.py:27
  110.7 69.0 %collective-permute-start.20 = (bf16[128,3072]{1,0:T(8,128)(2,1)S(1)}, bf16[128,3072]{1,0:T(8,128)(2,1)S(1)}, u32[]{:S(2)}, u32[]{:S(2)}) collective-permute-start(bf16[128,3072]{1,0:T(8,128)(2,1)S(1)} %add_convert_fusion), channel_id=1, source_target_pairs={{0,1},{1,2},{2,3},{3,4},{4,5},{5,6},{6,7},{7,8},{8,9},{9,10},{10,1... | collective-permute-start | bytes 2359304 | tf_op jit(solution)/shard_map/ppermute | solution.py:18
  111.0 56.2 %collective-permute-start.24 = (bf16[96,768]{1,0:T(8,128)(2,1)S(1)}, bf16[96,768]{1,0:T(8,128)(2,1)S(1)}, u32[]{:S(2)}, u32[]{:S(2)}) collective-permute-start(bf16[96,768]{1,0:T(8,128)(2,1)S(1)} %get-tuple-element.28), channel_id=1, source_target_pairs={{0,2},{2,0},{1,3},{3,1},{4,6},{6,4},{5,7},{7,5},{8,10},{10,8},{9,1... | collective-permute-start | bytes 442376 | tf_op jit(solution)/shard_map/ppermute | solution.py:27
  111.7 34.6 %collective-permute-start.27 = (bf16[96,768]{1,0:T(8,128)(2,1)S(1)}, bf16[96,768]{1,0:T(8,128)(2,1)S(1)}, u32[]{:S(2)}, u32[]{:S(2)}) collective-permute-start(bf16[96,768]{1,0:T(8,128)(2,1)S(1)} %get-tuple-element.32), channel_id=1, source_target_pairs={{0,2},{2,0},{1,3},{3,1},{4,6},{6,4},{5,7},{7,5},{8,10},{10,8},{9,1... | collective-permute-start | bytes 442376 | tf_op jit(solution)/shard_map/ppermute | solution.py:27
  113.1 17.2 %collective-permute-start.28 = (bf16[96,768]{1,0:T(8,128)(2,1)S(1)}, bf16[96,768]{1,0:T(8,128)(2,1)S(1)}, u32[]{:S(2)}, u32[]{:S(2)}) collective-permute-start(bf16[96,768]{1,0:T(8,128)(2,1)S(1)} %get-tuple-element.34), channel_id=1, source_target_pairs={{0,2},{2,0},{1,3},{3,1},{4,6},{6,4},{5,7},{7,5},{8,10},{10,8},{9,1... | collective-permute-start | bytes 442376 | tf_op jit(solution)/shard_map/ppermute | solution.py:27
  113.7 59.7 %collective-permute-start.31 = (bf16[96,768]{1,0:T(8,128)(2,1)S(1)}, bf16[96,768]{1,0:T(8,128)(2,1)S(1)}, u32[]{:S(2)}, u32[]{:S(2)}) collective-permute-start(bf16[96,768]{1,0:T(8,128)(2,1)S(1)} %get-tuple-element.36), channel_id=1, source_target_pairs={{0,2},{2,0},{1,3},{3,1},{4,6},{6,4},{5,7},{7,5},{8,10},{10,8},{9,1... | collective-permute-start | bytes 442376 | tf_op jit(solution)/shard_map/ppermute | solution.py:27
  143.8 9.6 %collective-permute-start.29 = (bf16[96,768]{1,0:T(8,128)(2,1)S(1)}, bf16[96,768]{1,0:T(8,128)(2,1)S(1)}, u32[]{:S(2)}, u32[]{:S(2)}) collective-permute-start(bf16[96,768]{1,0:T(8,128)(2,1)S(1)} %add_convert_fusion.6), channel_id=1, source_target_pairs={{0,8},{8,0},{1,9},{9,1},{2,10},{10,2},{3,11},{11,3},{4,12},{12,4},... | collective-permute-start | bytes 442376 | tf_op jit(solution)/shard_map/ppermute | solution.py:27
  153.4 13.8 %collective-permute-start.36 = (bf16[96,768]{1,0:T(8,128)(2,1)S(1)}, bf16[96,768]{1,0:T(8,128)(2,1)S(1)}, u32[]{:S(2)}, u32[]{:S(2)}) collective-permute-start(bf16[96,768]{1,0:T(8,128)(2,1)S(1)} %add_convert_fusion.3), channel_id=1, source_target_pairs={{0,8},{8,0},{1,9},{9,1},{2,10},{10,2},{3,11},{11,3},{4,12},{12,4},... | collective-permute-start | bytes 442376 | tf_op jit(solution)/shard_map/ppermute | solution.py:27
  153.5 19.8 %collective-permute-start.26 = (bf16[96,768]{1,0:T(8,128)(2,1)S(1)}, bf16[96,768]{1,0:T(8,128)(2,1)S(1)}, u32[]{:S(2)}, u32[]{:S(2)}) collective-permute-start(bf16[96,768]{1,0:T(8,128)(2,1)S(1)} %add_convert_fusion.7), channel_id=1, source_target_pairs={{0,8},{8,0},{1,9},{9,1},{2,10},{10,2},{3,11},{11,3},{4,12},{12,4},... | collective-permute-start | bytes 442376 | tf_op jit(solution)/shard_map/ppermute | solution.py:27
  167.2 7.7 %collective-permute-start.33 = (bf16[96,768]{1,0:T(8,128)(2,1)S(1)}, bf16[96,768]{1,0:T(8,128)(2,1)S(1)}, u32[]{:S(2)}, u32[]{:S(2)}) collective-permute-start(bf16[96,768]{1,0:T(8,128)(2,1)S(1)} %add_convert_fusion.4), channel_id=1, source_target_pairs={{0,8},{8,0},{1,9},{9,1},{2,10},{10,2},{3,11},{11,3},{4,12},{12,4},... | collective-permute-start | bytes 442376 | tf_op jit(solution)/shard_map/ppermute | solution.py:27
  167.3 9.3 %collective-permute-start.30 = (bf16[96,768]{1,0:T(8,128)(2,1)S(1)}, bf16[96,768]{1,0:T(8,128)(2,1)S(1)}, u32[]{:S(2)}, u32[]{:S(2)}) collective-permute-start(bf16[96,768]{1,0:T(8,128)(2,1)S(1)} %add_convert_fusion.5), channel_id=1, source_target_pairs={{0,4},{4,0},{1,5},{5,1},{2,6},{6,2},{3,7},{7,3},{8,12},{12,8},{9,1... | collective-permute-start | bytes 442376 | tf_op jit(solution)/shard_map/ppermute | solution.py:27
  (24 other events, 144.4 us)
